TPU v7x, 128 devices: a whole 4x4x4 slice. The times are simulated.
128 devices in a mesh: rep: 4 (over y), dp: 32 (over z, x, core).
Axes of the slice: x: 4, y: 4, z: 4, core: 2. Of those that a mesh axis runs over, the one named last changes fastest.
Arguments:
- gradient: bfloat16 [4, 64, 512, 512], P('rep', None, 'dp')
- owner: int32 [64, 1], replicated, may hold values from 0 to 31; in each aligned block of 64 rows (0 to 63, 64 to 127, ...) at most 4 rows name the same one
- left_factor: float32 [128, 512, 512], P('dp'), as said below
- right_factor: float32 [128, 512, 512], P('dp'), as said below
- left_root: bfloat16 [128, 512, 512], P('dp'), as said below
- right_root: bfloat16 [128, 512, 512], P('dp'), as said below
Outputs:
- update: bfloat16 [64, 512, 512], P(None, 'dp')
- left_out: float32 [128, 512, 512], P('dp')
- right_out: float32 [128, 512, 512], P('dp')
Inputs may be any that keep to these rules, and one draw needn't show every extreme that they name: `owner`: every dp index owns 1 to 4 blocks and some index owns exactly 4. `left_factor`: symmetric in the last two dimensions. `right_factor`: symmetric in the last two dimensions. `left_root`: symmetric in the last two dimensions. `right_root`: symmetric in the last two dimensions.
All inputs are finite; a program needn't handle non-finite values.
Results may differ from a plain program's by a relative error of at most 0.018.
Values may be sent and summed in bfloat16 or wider, within the bound.
A program may use at most 128 MiB of HBM per device.

v0:
```python
import jax
import jax.numpy as jnp
from jax import lax
from jax.sharding import PartitionSpec as P

CAP = 4


DECAY = 0.9
EPS = 1e-06


def slot_tables(owner_ids, devices, capacity):
    count = owner_ids.shape[0]
    position = jnp.arange(count, dtype=jnp.int32)
    same = owner_ids[:, None] == owner_ids[None, :]
    earlier = position[None, :] < position[:, None]
    slot = jnp.sum((same & earlier).astype(jnp.int32), axis=1)
    flat = slot * devices + owner_ids
    table = (flat[None, :] == jnp.arange(capacity * devices, dtype=jnp.int32)[:, None]).astype(
        jnp.int32
    )
    live = jnp.sum(table, axis=1)
    source = jnp.sum(table * position[None, :], axis=1)
    return (flat, source, live)


def owner_work(blocks, left, right, left_inv, right_inv):
    width = blocks.shape[1]
    high = lax.Precision.HIGHEST
    left_new = DECAY * left + (1.0 - DECAY) / width * jnp.einsum(
        "nij,nkj->nik", blocks, blocks, precision=high, preferred_element_type=jnp.float32
    )
    right_new = DECAY * right + (1.0 - DECAY) / width * jnp.einsum(
        "nji,njk->nik", blocks, blocks, precision=high, preferred_element_type=jnp.float32
    )
    grad_low = blocks.astype(jnp.bfloat16)
    half = jnp.einsum(
        "nij,njk->nik", left_inv, grad_low, preferred_element_type=jnp.float32
    ).astype(jnp.bfloat16)
    direction = jnp.einsum("nij,njk->nik", half, right_inv, preferred_element_type=jnp.float32)
    grad_norm = jnp.sqrt(jnp.sum(blocks * blocks, axis=(1, 2), keepdims=True))
    dir_norm = jnp.sqrt(jnp.sum(direction * direction, axis=(1, 2), keepdims=True) + EPS)
    steps = (direction * (grad_norm / dir_norm)).astype(jnp.bfloat16)
    return (left_new, right_new, steps)


def shards(gradient, owner, left_factor, right_factor, left_root, right_root):
    devices = lax.axis_size("dp")
    rows_local = gradient.shape[2]
    width = gradient.shape[3]
    flat, source, live = slot_tables(owner[:, 0], devices, CAP)
    summed = lax.psum(gradient[0].astype(jnp.float32).astype(jnp.bfloat16), "rep").astype(
        jnp.float32
    )
    picked = jnp.take(summed, source, axis=0) * live.astype(jnp.float32)[:, None, None]
    outgoing = picked.reshape(CAP, devices, rows_local, width)
    arrived = lax.all_to_all(
        outgoing.astype(jnp.bfloat16), "dp", split_axis=1, concat_axis=1, tiled=True
    ).astype(outgoing.dtype)
    blocks = arrived.reshape(CAP, width, width)
    left_out, right_out, steps = owner_work(
        blocks, left_factor, right_factor, left_root, right_root
    )
    homeward = steps.reshape(CAP, devices, rows_local, width)
    returned = lax.all_to_all(homeward, "dp", split_axis=1, concat_axis=1, tiled=True)
    update = jnp.take(returned.reshape(CAP * devices, rows_local, width), flat, axis=0)
    return (update, left_out, right_out)


def solution(mesh):
    in_specs = (
        P("rep", None, "dp", None),
        P(),
        P("dp", None, None),
        P("dp", None, None),
        P("dp", None, None),
        P("dp", None, None),
    )
    out_specs = (P(None, "dp", None), P("dp", None, None), P("dp", None, None))
    return jax.shard_map(shards, mesh=mesh, in_specs=in_specs, out_specs=out_specs, check_vma=False)
```

profile of v0, /device:TPU:1, one launch (start us, length us, event | category | flops | bytes accessed | tf_op | source)
XLA Modules:
  0.0 167.8 jit_solution(11746278160993518385)
XLA Ops:
  7.2 0.0 copy-start
  7.2 0.0 all-reduce.2.cloned.1.call-start
  7.2 0.7 all-reduce.2.cloned.1.call-update
  7.9 0.9 convert_reduce_fusion.1
  8.8 0.7 multiply_add_fusion.2
  9.5 0.1 convert_reduce_fusion
  9.6 0.1 reduce_sum.51
  9.7 0.1 convert_element_type.42
  9.8 48.2 %all-reduce.2.cloned.1.call-done = bf16[64,16,512]{2,1,0:T(8,128)(2,1)} async-done(((bf16[64,16,512]{2,1,0:T(8,128)(2,1)}), bf16[64,16,512]{2,1,0:T(8,128)(2,1)}) %all-reduce.2.cloned.1.call-update) | async-done | bytes 1048592 | tf_op jit(solution)/shard_map/psum | solution.py:53
  58.0 2.8 %convert_element_type.39 = f32[64,16,512]{2,1,0:T(8,128)} convert(bf16[64,16,512]{2,1,0:T(8,128)(2,1)} %all-reduce.2.cloned.1.call-done) | non-fusion elementwise | flops 524288 | bytes 3145728 | tf_op jit(solution)/shard_map/convert_element_type | solution.py:53
  60.9 4.4 %gather_fusion = f32[128,16,512]{2,1,0:T(8,128)} fusion(f32[64,16,512]{2,1,0:T(8,128)} %convert_element_type.39, s32[1024]{0:T(1024)S(1)} %pad_clamp_fusion.1), kind=kCustom, calls=%fused_computation | custom fusion | bytes 8389120 | tf_op jit(solution)/shard_map/jit(_take)/gather | solution.py:56
  65.3 2.6 %multiply_convert_fusion.1 = bf16[4,32,16,512]{3,2,1,0:T(8,128)(2,1)S(1)} fusion(f32[4,32,16,512]{3,2,1,0:T(8,128)} %bitcast.29, f32[4,32]{1,0:T(4,128)S(1)} %convert_element_type.42, pred[4,32]{1,0:T(4,128)(4,1)S(1)} %compare_and_fusion), kind=kLoop, calls=%fused_computation.7 | loop fusion | flops 3145728 | bytes 6292096 | tf_op jit(solution)/shard_map/convert_element_type | solution.py:59
  67.9 0.2 copy.27
  68.1 37.3 %all_to_all.10 = bf16[4,32,16,512]{3,2,0,1:T(8,128)(2,1)S(1)} all-to-all(bf16[4,32,16,512]{3,2,0,1:T(8,128)(2,1)S(1)} %copy.27), channel_id=1, replica_groups=mesh['rep'=4,'dp'=32] {'dp'}, dimensions={1} | all-to-all | bytes 4194304 | tf_op jit(solution)/shard_map/all_to_all | solution.py:58
  105.4 0.0 copy-start.2
  105.4 1.3 copy-done.2
  106.7 1.5 copy.28
  108.3 0.0 copy-done
  108.3 6.8 %multiply_reduce_fusion = (f32[4]{0:T(128)S(1)}, f32[4,512,512]{2,1,0:T(8,128)}) fusion(bf16[4,512,512]{2,1,0:T(8,128)(2,1)S(1)} %copy-done, bf16[4,512,512]{2,1,0:T(8,128)(2,1)} %bitcast.26, bf16[4,512,512]{2,1,0:T(8,128)(2,1)} %param.10), kind=kOutput, calls=%fused_computation.5 | convolution fusion | flops 2150629376 | bytes 10485776 | tf_op jit(solution)/shard_map/nij,njk->nik/dot_general | solution.py:41
  115.0 2.2 %multiply_reduce_fusion.1 = f32[4]{0:T(128)S(1)} fusion(bf16[4,32,16,512]{3,2,0,1:T(8,128)(2,1)} %copy-done.2), kind=kLoop, calls=%fused_computation.6 | loop fusion | flops 3145724 | bytes 2097168 | tf_op jit(solution)/shard_map/reduce_sum | solution.py:42
  117.3 2.8 %multiply_convert_fusion = bf16[4,512,512]{2,1,0:T(8,128)(2,1)S(1)} fusion(f32[4,512,512]{2,1,0:T(8,128)} %get-tuple-element.8, f32[4]{0:T(128)S(1)} %rsqrt_multiply_fusion), kind=kLoop, calls=%fused_computation.4 | loop fusion | flops 2097152 | bytes 6291472 | tf_op jit(solution)/shard_map/convert_element_type | solution.py:44
  120.1 1.5 copy.31
  121.6 0.0 copy-start.4
  121.6 4.9 %all-to-all-start.1 = ((bf16[4,32,16,512]{3,2,0,1:T(8,128)(2,1)}), bf16[4,32,16,512]{3,2,0,1:T(8,128)(2,1)}, u32[]{:S(2)}, u32[]{:S(2)}) async-start(bf16[4,32,16,512]{3,2,0,1:T(8,128)(2,1)} %copy.31), calls=%async_computation.1 | async-start | bytes 4194304 | tf_op jit(solution)/shard_map/all_to_all | solution.py:66
  126.5 0.0 copy-done.4
  126.5 0.0 copy-start.1
  126.6 0.0 copy-start.3
  126.6 7.1 %multiply_add_fusion = f32[4,512,512]{2,1,0:T(8,128)} fusion(f32[4,512,512]{2,1,0:T(8,128)} %param.9, bf16[4,512,512]{2,1,0:T(8,128)(2,1)} %bitcast.27), kind=kOutput, calls=%fused_computation.2 | convolution fusion | flops 1076887552 | bytes 10485760 | tf_op jit(solution)/shard_map/nji,njk->nik/dot_general | solution.py:34
  133.7 0.0 copy-done.1
  133.7 0.0 copy-done.3
  133.7 3.4 %multiply_add_fusion.1 = f32[4,512,512]{2,1,0:T(8,128)} fusion(f32[4,512,512]{2,1,0:T(8,128)S(1)} %copy-done.3, bf16[4,512,512]{2,1,0:T(8,128)(2,1)S(1)} %bitcast.28), kind=kOutput, calls=%fused_computation.3 | convolution fusion | flops 1076887552 | bytes 10485760 | tf_op jit(solution)/shard_map/nij,nkj->nik/dot_general | solution.py:31
  137.1 17.4 %all-to-all-done.1 = bf16[4,32,16,512]{3,2,0,1:T(8,128)(2,1)} async-done(((bf16[4,32,16,512]{3,2,0,1:T(8,128)(2,1)}), bf16[4,32,16,512]{3,2,0,1:T(8,128)(2,1)}, u32[]{:S(2)}, u32[]{:S(2)}) %all-to-all-start.1) | async-done | bytes 2097184 | tf_op jit(solution)/shard_map/all_to_all | solution.py:66
  154.5 3.1 %copy.32 = bf16[4,32,16,512]{3,2,1,0:T(8,128)(2,1)} copy(bf16[4,32,16,512]{3,2,0,1:T(8,128)(2,1)} %all-to-all-done.1) | data formatting | bytes 4194304 | tf_op jit(solution)/shard_map/all_to_all | solution.py:66
  157.6 2.2 %gather_fusion.1 = bf16[64,16,512]{2,1,0:T(8,128)(2,1)S(1)} fusion(bf16[128,16,512]{2,1,0:T(8,128)(2,1)} %bitcast.31, s32[1024]{0:T(1024)S(1)} %pad_clamp_fusion), kind=kCustom, calls=%fused_computation.1 | custom fusion | bytes 2097408 | tf_op jit(solution)/shard_map/jit(_take)/gather | solution.py:67
  159.8 1.1 broadcast_select_fusion
  (7 shorter events, 0.0 us)
Async XLA Ops:
  7.2 101.1 %copy-start = (bf16[4,512,512]{2,1,0:T(8,128)(2,1)S(1)}, bf16[4,512,512]{2,1,0:T(8,128)(2,1)}, u32[]{:S(2)}) copy-start(bf16[4,512,512]{2,1,0:T(8,128)(2,1)} %param.11) | copy-start | bytes 6291460
  7.2 50.8 %all-reduce.2.cloned.1.call-start = ((), (), s32[]{:S(2)}) async-start(), calls=%async_computation.2 | async-start | bytes 2097152 | tf_op jit(solution)/shard_map/psum | solution.py:53
  105.4 1.4 copy-start.2
  121.6 4.9 %copy-start.4 = (s32[64,1]{0,1:T(1,128)S(1)}, s32[64,1]{0,1:T(1,128)}, u32[]{:S(2)}) copy-start(s32[64,1]{0,1:T(1,128)} %param.7) | copy-start | bytes 772
  121.6 32.9 %all-to-all-start.1 = ((bf16[4,32,16,512]{3,2,0,1:T(8,128)(2,1)}), bf16[4,32,16,512]{3,2,0,1:T(8,128)(2,1)}, u32[]{:S(2)}, u32[]{:S(2)}) async-start(bf16[4,32,16,512]{3,2,0,1:T(8,128)(2,1)} %copy.31), calls=%async_computation.1 | async-start | bytes 4194304 | tf_op jit(solution)/shard_map/all_to_all | solution.py:66
  126.5 7.1 %copy-start.1 = (bf16[4,32,16,512]{3,2,1,0:T(8,128)(2,1)S(1)}, bf16[4,32,16,512]{3,2,1,0:T(8,128)(2,1)}, u32[]{:S(2)}) copy-start(bf16[4,32,16,512]{3,2,1,0:T(8,128)(2,1)} %copy.28) | copy-start | bytes 6291460
  126.6 7.1 %copy-start.3 = (f32[4,512,512]{2,1,0:T(8,128)S(1)}, f32[4,512,512]{2,1,0:T(8,128)}, u32[]{:S(2)}) copy-start(f32[4,512,512]{2,1,0:T(8,128)} %param.8) | copy-start | bytes 12582916
Sparse Core Ops, SparseCore 0:
  10.4 47.5 all-reduce.1
where the time goes:
time: 169 us; the launch traced here: 168 us
  waiting for transfers between devices  66.3 us (39%)
  blocking collectives  37.3 us (22%)
  matrix products  17.3 us (10%)
  local copies, waits for them, and re-layouts  14.5 us (9%)
  between operations  14.1 us (8%)
  other arithmetic  13.4 us (8%)
  starting transfers between devices  4.9 us (3%)
    psum x1, waiting for transfers between devices, shards(): lax.psum(gradient[0].astype(jnp.float32).astype(jnp.bfloat16), 'rep')  48.2 us
    all_to_all x1, blocking collectives, shards(): lax.all_to_all(outgoing.astype(jnp.bfloat16), 'dp', split_axis=1, concat_...  37.3 us
    all_to_all x1, waiting for transfers between devices, shards(): lax.all_to_all(homeward, 'dp', split_axis=1, concat_axis=1, tiled=True)  17.4 us
    dot_general x1, matrix products, owner_work(): jnp.einsum('nji,njk->nik', blocks, blocks, precision=high, preferred_elem...  7.11 us
    dot_general x1, matrix products, owner_work(): jnp.einsum('nij,njk->nik', half, right_inv, preferred_element_type=jnp.fl...  6.78 us
    all_to_all x1, starting transfers between devices, shards(): lax.all_to_all(homeward, 'dp', split_axis=1, concat_axis=1, tiled=True)  4.87 us
    gather x1, local copies, waits for them, and re-layouts, shards(): jnp.take(summed, source, axis=0) * live.astype(jnp.float32)[:, None, None]  4.42 us
    dot_general x1, matrix products, owner_work(): jnp.einsum('nij,nkj->nik', blocks, blocks, precision=high, preferred_elem...  3.44 us
  transfers between devices with their start and end apart: 2, of which 2 were waited for; matrix products, arithmetic and copies ran while one was open for 7% of the time, Pallas kernels for 0%

commit v1 on v0

v1 whole, which is shorter than its diff:
```python
import functools

import jax
import jax.numpy as jnp
from jax import lax
from jax.experimental import pallas as pl
from jax.experimental.pallas import tpu as pltpu
from jax.sharding import PartitionSpec as P

MESH = pl.DeviceIdType.MESH
CAP = 4
DECAY = 0.9
EPS = 1e-06
CHUNKS = 2
STEPS = (1, 3, 2)
TAB_ROWS = 16
ROW_BLOCK, ROW_POS, ROW_OWNER, ROW_START, ROW_COUNT, ROW_PLACE = 0, 1, 2, 3, 4, 5


def in_vmem(shape, dtype):
    return pltpu.VMEM(shape, dtype)


def from_vmem(x):
    return pltpu.with_memory_space_constraint(x, pltpu.VMEM)


def fill_tables(owner_ref, tab_ref):
    blocks = owner_ref.shape[1]
    lanes = tab_ref.shape[1]
    b = lax.broadcasted_iota(jnp.int32, (blocks, lanes), 0)
    c = lax.broadcasted_iota(jnp.int32, (blocks, lanes), 1)

    def down(x):
        return jnp.sum(x, axis=0, keepdims=True)

    inside = c < blocks
    row = jnp.broadcast_to(jnp.pad(owner_ref[...], ((0, 0), (0, lanes - blocks))), (blocks, lanes))
    col = jnp.sum(jnp.where(b == c, row, 0), axis=1, keepdims=True)
    col = jnp.broadcast_to(col, (blocks, lanes))
    before = (row < col) | ((row == col) & (c < b))
    pos_col = jnp.sum(jnp.where(before & inside, 1, 0), axis=1, keepdims=True)
    pos_col = jnp.broadcast_to(pos_col, (blocks, lanes))
    after = (col < row) | ((col == row) & (b < c))
    pos_row = down(jnp.where(after, 1, 0))
    here = pos_col == c
    start = down(jnp.where(col < c, 1, 0))
    count = down(jnp.where(col == c, 1, 0))
    tab_ref[ROW_BLOCK : ROW_BLOCK + 1, :] = down(jnp.where(here, b, 0))
    tab_ref[ROW_POS : ROW_POS + 1, :] = pos_row
    tab_ref[ROW_OWNER : ROW_OWNER + 1, :] = down(jnp.where(here, col, 0))
    tab_ref[ROW_START : ROW_START + 1, :] = start
    tab_ref[ROW_COUNT : ROW_COUNT + 1, :] = count
    for q in range(CAP):
        slot = (q - start) & 3
        place = jnp.where(slot < count, (start + slot) >> 2, 0)
        tab_ref[ROW_PLACE + q : ROW_PLACE + q + 1, :] = place
    rest = ROW_PLACE + CAP
    tab_ref[rest:, :] = jnp.zeros((TAB_ROWS - rest, lanes), jnp.int32)


def exchange(
    reps, devs, owner_ref, grad_hbm, lf_hbm, rf_hbm, lr_hbm, rr_hbm,
    tab_out, gath, uall, lf_out, rf_out,
    tab, grad, lroot, rroot, rs_send, rs_recv, stage, half, direct, upd, s_own, s_recv, back,
    loc_sem, rs_ss, rs_rs, ag_ss, ag_rs, pr_ss, pr_rs, ot_ss, ot_rs, bk_ss, bk_rs, au_ss, au_rs,
):
    r = lax.axis_index("rep")
    d = lax.axis_index("dp")
    places, rows, width = s_own[0].shape[0], grad.shape[1], grad.shape[2]
    part = width // CHUNKS
    cols = [pl.ds(c * part, part) for c in range(CHUNKS)]
    tile = min(256, width)
    mine = pl.ds(pl.multiple_of(d * rows, rows), rows)

    def rep_peer(k):
        return (lax.rem(r + k, reps), d)

    def dp_peer(t):
        return lax.rem(d + t, devs)

    def local(src, dst, i):
        return pltpu.make_async_copy(src, dst, loc_sem.at[i])

    loads = [
        local(grad_hbm, grad, 0),
        local(lr_hbm, lroot, 1),
        local(rr_hbm, rroot, 2),
        local(lf_hbm, lf_out, 3),
        local(rf_hbm, rf_out, 4),
    ]
    for load in loads:
        load.start()

    barrier = pltpu.get_barrier_semaphore()
    for k in STEPS:
        pl.semaphore_signal(barrier, inc=1, device_id=rep_peer(k), device_id_type=MESH)

    def greet(t, carry):
        pl.semaphore_signal(barrier, inc=1, device_id=(r, dp_peer(t)), device_id_type=MESH)
        return carry

    lax.fori_loop(1, devs, greet, 0)

    fill_tables(owner_ref, tab_out)
    to_scalars = local(tab_out, tab, 5)
    to_scalars.start()
    to_scalars.wait()
    loads[0].wait()

    for i, k in enumerate(STEPS):
        q = lax.rem(r + k, reps)

        def pack(j, carry, i=i, q=q):
            block = tab[ROW_BLOCK, CAP * j + q]
            for c in range(CHUNKS):
                rs_send[c, i, j] = grad[block, :, cols[c]]
            return carry

        lax.fori_loop(0, places, pack, 0)

    pl.semaphore_wait(barrier, reps - 1 + devs - 1)

    def over_rep(src, dst, ss, rs):
        copies = []
        for i, k in enumerate(STEPS):
            copies.append(
                pltpu.make_async_remote_copy(
                    src_ref=src(i),
                    dst_ref=dst(i),
                    send_sem=ss.at[i],
                    recv_sem=rs.at[i],
                    device_id=rep_peer(k),
                    device_id_type=MESH,
                )
            )
        for copy in copies:
            copy.start()
        return copies

    rs = [
        over_rep(lambda i: rs_send.at[c, i], lambda i: rs_recv.at[c, i], rs_ss.at[c], rs_rs.at[c])
        for c in range(CHUNKS)
    ]

    def one(src, dst, ss, rs, to):
        pltpu.make_async_remote_copy(
            src_ref=src, dst_ref=dst, send_sem=ss, recv_sem=rs, device_id=(r, to), device_id_type=MESH
        ).start()

    ag = []
    for c in range(CHUNKS):
        for copy in rs[c]:
            copy.wait_recv()

        def add(j, carry, c=c):
            block = tab[ROW_BLOCK, CAP * j + r]
            total = grad[block, :, cols[c]].astype(jnp.float32)
            for i in range(len(STEPS)):
                total += rs_recv[c, i, j].astype(jnp.float32)
            s_own[c][j] = total.astype(jnp.bfloat16)
            return carry

        lax.fori_loop(0, places, add, 0)

        def to_owner(t, carry, c=c):
            o = dp_peer(t)
            stage[0, o, :, cols[c]] = s_own[c][tab[ROW_PLACE + r, o]]
            one(stage.at[0, o, :, cols[c]], gath.at[0, mine, cols[c]], pr_ss.at[c], pr_rs.at[c], o)
            return carry

        lax.fori_loop(1, devs, to_owner, 0)
        gath[0, mine, cols[c]] = s_own[c][tab[ROW_PLACE + r, d]]
        ag.append(over_rep(lambda i: s_own[c], lambda i: s_recv[i].at[c], ag_ss.at[c], ag_rs.at[c]))

    slot = (r - tab[ROW_START, d]) & 3
    loads[1].wait()
    loads[2].wait()
    for c in range(CHUNKS):
        arrived = gath.at[0, pl.ds(0, rows * (devs - 1)), cols[c]]
        pltpu.make_async_copy(arrived, arrived, pr_rs.at[c]).wait()
        for m in range(0, width, tile):
            half[m : m + tile, cols[c]] = jnp.dot(
                lroot[slot, m : m + tile, :], gath[0, :, cols[c]], preferred_element_type=jnp.float32
            ).astype(jnp.bfloat16)
    grad_sq = jnp.zeros((1, 1), jnp.float32)
    dir_sq = jnp.zeros((1, 1), jnp.float32)
    for m in range(0, width, tile):
        piece = jnp.dot(half[m : m + tile, :], rroot[slot], preferred_element_type=jnp.float32)
        direct[m : m + tile, :] = piece
        dir_sq += jnp.sum(piece * piece, keepdims=True)
        g = gath[0, m : m + tile, :].astype(jnp.float32)
        grad_sq += jnp.sum(g * g, keepdims=True)
    scale = jnp.sqrt(grad_sq) / jnp.sqrt(dir_sq + EPS)
    for m in range(0, width, tile):
        upd[m : m + tile, :] = (direct[m : m + tile, :] * scale).astype(jnp.bfloat16)

    for c in range(CHUNKS):

        def homeward(t, carry, c=c):
            to = dp_peer(t)
            theirs = pl.ds(pl.multiple_of(to * rows, rows), rows)
            one(upd.at[theirs, cols[c]], back[c].at[d], bk_ss.at[c], bk_rs.at[c], to)
            return carry

        lax.fori_loop(1, devs, homeward, 0)
        back[c][d] = upd[mine, cols[c]]

    for i, k in enumerate(STEPS):
        for c in range(CHUNKS):
            ag[c][i].wait_recv()
        q = lax.rem(r + reps - k, reps)

        def to_owner_too(t, carry, i=i, q=q):
            o = dp_peer(t)
            place = tab[ROW_PLACE + q, o]
            for c in range(CHUNKS):
                stage[1 + i, o, :, cols[c]] = s_recv[i][c, place]
            one(stage.at[1 + i, o], gath.at[1 + i, mine, :], ot_ss.at[i], ot_rs.at[i], o)
            return carry

        lax.fori_loop(1, devs, to_owner_too, 0)
        own = tab[ROW_PLACE + q, d]
        for c in range(CHUNKS):
            gath[1 + i, mine, cols[c]] = s_recv[i][c, own]

    au = []
    for c in range(CHUNKS):
        arrived = back[c].at[pl.ds(0, devs - 1)]
        pltpu.make_async_copy(arrived, arrived, bk_rs.at[c]).wait()

        def unpack(j, carry, c=c):
            uall[0, j, :, cols[c]] = back[c][tab[ROW_OWNER, CAP * j + r]]
            return carry

        lax.fori_loop(0, places, unpack, 0)
        au.append(
            over_rep(
                lambda i: uall.at[0, :, :, cols[c]],
                lambda i: uall.at[1 + i, :, :, cols[c]],
                au_ss.at[c],
                au_rs.at[c],
            )
        )

    for c in range(CHUNKS):
        for copy in rs[c] + ag[c]:
            copy.wait_send()
        sent = stage.at[0, pl.ds(0, devs - 1), :, cols[c]]
        pltpu.make_async_copy(sent, sent, pr_ss.at[c]).wait()
        sent = back[c].at[pl.ds(0, devs - 1)]
        pltpu.make_async_copy(sent, sent, bk_ss.at[c]).wait()
    for i in range(len(STEPS)):
        sent = stage.at[1 + i, pl.ds(0, devs - 1)]
        pltpu.make_async_copy(sent, sent, ot_ss.at[i]).wait()
        arrived = gath.at[1 + i, pl.ds(0, rows * (devs - 1)), :]
        pltpu.make_async_copy(arrived, arrived, ot_rs.at[i]).wait()
    for copies in au:
        for copy in copies:
            copy.wait()
    loads[3].wait()
    loads[4].wait()


def write_out(
    reps, tab_v, gath, uall, lf, rf, update, left_out, right_out, tab, left_buf, right_buf, sems
):
    r = lax.axis_index("rep")
    d = lax.axis_index("dp")
    blocks, width = update.shape[0], gath.shape[2]
    places = uall.shape[1]
    tile = min(256, width)
    load = pltpu.make_async_copy(tab_v, tab, sems.at[0])
    load.start()
    load.wait()

    def buffer_of(q):
        step = lax.rem(r - q + reps, reps)
        return jnp.where(step < 2, step, 5 - step)

    def put(b, carry):
        pos = tab[ROW_POS, b]
        pltpu.make_async_copy(uall.at[buffer_of(pos & 3), pos >> 2], update.at[b], sems.at[1]).start()
        return carry

    lax.fori_loop(0, blocks, put, 0)
    start, count = tab[ROW_START, d], tab[ROW_COUNT, d]
    weight = (1.0 - DECAY) / width
    copies = []
    for s in range(CAP):
        valid = s < count
        idx = buffer_of((start + s) & 3)
        for side, (factor, buf, out) in enumerate(((lf, left_buf, left_out), (rf, right_buf, right_out))):
            for m in range(0, width, tile):
                sl = pl.ds(m, tile)
                if side == 0:
                    gram = lax.dot_general(
                        gath[idx, sl, :], gath[idx], (((1,), (1,)), ((), ())), preferred_element_type=jnp.float32
                    )
                else:
                    gram = lax.dot_general(
                        gath[idx, :, sl], gath[idx], (((0,), (0,)), ((), ())), preferred_element_type=jnp.float32
                    )
                buf[s, sl, :] = DECAY * factor[s, sl, :] + jnp.where(valid, weight * gram, 0.0)
                copy = pltpu.make_async_copy(buf.at[s, sl], out.at[s, sl], sems.at[2])
                copy.start()
                copies.append(copy)
    pltpu.make_async_copy(left_buf, left_out, sems.at[2]).wait()
    pltpu.make_async_copy(right_buf, right_out, sems.at[2]).wait()
    flat = uall
    pltpu.make_async_copy(flat, flat, sems.at[1]).wait()


def shards(reps, devs, gradient, owner, left_factor, right_factor, left_root, right_root):
    bf16, f32 = jnp.bfloat16, jnp.float32
    _, blocks, rows, width = gradient.shape
    places = blocks // reps
    part = width // CHUNKS
    any_spec = pl.BlockSpec(memory_space=pl.ANY)
    vmem_spec = pl.BlockSpec(memory_space=pltpu.VMEM)
    dma = pltpu.SemaphoreType.DMA
    three = len(STEPS)
    tab, gath, uall, lf, rf = pl.pallas_call(
        functools.partial(exchange, reps, devs),
        name="exchange",
        out_shape=[
            in_vmem((TAB_ROWS, 128), jnp.int32),
            in_vmem((CAP, width, width), bf16),
            in_vmem((CAP, places, rows, width), bf16),
            in_vmem((CAP, width, width), f32),
            in_vmem((CAP, width, width), f32),
        ],
        in_specs=[vmem_spec] + [any_spec] * 5,
        out_specs=[vmem_spec] * 5,
        scratch_shapes=[
            pltpu.SMEM((TAB_ROWS, 128), jnp.int32),
            pltpu.VMEM((blocks, rows, width), bf16),
            pltpu.VMEM((CAP, width, width), bf16),
            pltpu.VMEM((CAP, width, width), bf16),
            pltpu.VMEM((CHUNKS, three, places, rows, part), bf16),
            pltpu.VMEM((CHUNKS, three, places, rows, part), bf16),
            pltpu.VMEM((CAP, devs, rows, width), bf16),
            pltpu.VMEM((width, width), bf16),
            pltpu.VMEM((width, width), f32),
            pltpu.VMEM((width, width), bf16),
            [pltpu.VMEM((places, rows, part), bf16)] * CHUNKS,
            [pltpu.VMEM((CHUNKS, places, rows, part), bf16)] * three,
            [pltpu.VMEM((devs, rows, part), bf16)] * CHUNKS,
            dma((6,)),
            dma((CHUNKS, three)),
            dma((CHUNKS, three)),
            dma((CHUNKS, three)),
            dma((CHUNKS, three)),
            dma((CHUNKS,)),
            dma((CHUNKS,)),
            dma((three,)),
            dma((three,)),
            dma((CHUNKS,)),
            dma((CHUNKS,)),
            dma((CHUNKS, three)),
            dma((CHUNKS, three)),
        ],
        compiler_params=pltpu.CompilerParams(
            collective_id=0, has_side_effects=True, vmem_limit_bytes=40 * 2**20
        ),
    )(owner.reshape(1, blocks), gradient[0], left_factor, right_factor, left_root, right_root)
    update, left_out, right_out = pl.pallas_call(
        functools.partial(write_out, reps),
        name="write_out",
        out_shape=[
            jax.ShapeDtypeStruct((blocks, rows, width), bf16),
            jax.ShapeDtypeStruct((CAP, width, width), f32),
            jax.ShapeDtypeStruct((CAP, width, width), f32),
        ],
        in_specs=[any_spec] + [vmem_spec] * 4,
        out_specs=[pl.BlockSpec(memory_space=pltpu.HBM)] * 3,
        scratch_shapes=[
            pltpu.SMEM((TAB_ROWS, 128), jnp.int32),
            pltpu.VMEM((CAP, width, width), f32),
            pltpu.VMEM((CAP, width, width), f32),
            dma((3,)),
        ],
        compiler_params=pltpu.CompilerParams(vmem_limit_bytes=24 * 2**20),
    )(tab, *(from_vmem(x) for x in (gath, uall, lf, rf)))
    return update, left_out, right_out


def solution(mesh):
    in_specs = (
        P("rep", None, "dp", None),
        P(),
        P("dp", None, None),
        P("dp", None, None),
        P("dp", None, None),
        P("dp", None, None),
    )
    out_specs = (P(None, "dp", None), P("dp", None, None), P("dp", None, None))
    body = functools.partial(shards, mesh.shape["rep"], mesh.shape["dp"])
    return jax.shard_map(body, mesh=mesh, in_specs=in_specs, out_specs=out_specs, check_vma=False)
```

time: 169 us -> 63.9 us (0.38)
  waiting for transfers between devices: 66.3 us -> 0 us
  Pallas kernels: 0 us -> 61.2 us
  blocking collectives: 37.3 us -> 0 us
  matrix products: 17.3 us -> 0 us
  between operations: 14.1 us -> 0.65 us
  other arithmetic: 13.4 us -> 0 us
  local copies, waits for them, and re-layouts: 14.5 us -> 1.87 us
  starting transfers between devices: 4.9 us -> 0 us
    pallas_call x0 -> x2, Pallas kernels: none -> 61.2 us  [the longest x1 55.8 us: shards(): pl.pallas_call(functools.partial(exchange, reps, devs), name='exchange',...]
    psum x1 -> x0, waiting for transfers between devices: 48.2 us -> none  [shards(): lax.psum(gradient[0].astype(jnp.float32).astype(jnp.bfloat16), 'rep')]
    all_to_all x1 -> x0, blocking collectives: 37.3 us -> none  [shards(): lax.all_to_all(outgoing.astype(jnp.bfloat16), 'dp', split_axis=1, concat_...]
    all_to_all x1 -> x0, waiting for transfers between devices: 17.4 us -> none  [shards(): lax.all_to_all(homeward, 'dp', split_axis=1, concat_axis=1, tiled=True)]
    dot_general x3 -> x0, matrix products: 17.3 us -> none  [the longest x1 7.11 us: owner_work(): jnp.einsum('nji,njk->nik', blocks, blocks, precision=high, preferred_elem...]
    convert_element_type x4 -> x0, other arithmetic: 8.28 us -> none  [the longest x1 2.84 us: shards(): lax.psum(gradient[0].astype(jnp.float32).astype(jnp.bfloat16), 'rep')]
    gather x2 -> x0, local copies, waits for them, and re-layouts: 6.62 us -> none  [the longest x1 4.42 us: shards(): jnp.take(summed, source, axis=0) * live.astype(jnp.float32)[:, None, None]]
    all_to_all x1 -> x0, starting transfers between devices: 4.87 us -> none  [shards(): lax.all_to_all(homeward, 'dp', split_axis=1, concat_axis=1, tiled=True)]
  transfers between devices with their start and end apart: 2 -> 0, of which waited for: 2 -> 0; matrix products, arithmetic and copies ran while one was open for 7% -> 0% of each run, Pallas kernels for 0% -> 0%
where the time goes in v1:
time: 63.9 us; the launch traced here: 63.7 us
  Pallas kernels  61.2 us (96%)
  local copies, waits for them, and re-layouts  1.87 us (3%)
  between operations  0.65 us (1%)
    pallas_call x1, Pallas kernels, shards(): pl.pallas_call(functools.partial(exchange, reps, devs), name='exchange',...  55.8 us
    pallas_call x1, Pallas kernels, shards(): pl.pallas_call(functools.partial(write_out, reps), name='write_out', out_...  5.4 us
    unnamed x4, local copies, waits for them, and re-layouts  1.87 us

profile of v1, /device:TPU:1, one launch (start us, length us, event | category | flops | bytes accessed | tf_op | source)
XLA Modules:
  0.0 63.7 jit_solution(13584942523659634067)
XLA Ops:
  0.6 0.0 copy-start
  0.6 1.2 %copy-done = bf16[1,64,16,512]{3,2,1,0:T(8,128)(2,1)S(1)} copy-done((bf16[1,64,16,512]{3,2,1,0:T(8,128)(2,1)S(1)}, bf16[1,64,16,512]{3,2,1,0:T(8,128)(2,1)}, u32[]{:S(2)}) %copy-start) | copy-done | bytes 1048600
  1.9 0.0 copy-start.1
  1.9 0.7 %copy-done.1 = s32[64,1]{0,1:T(1,128)S(1)} copy-done((s32[64,1]{0,1:T(1,128)S(1)}, s32[64,1]{0,1:T(1,128)}, u32[]{:S(2)}) %copy-start.1) | copy-done | bytes 280
  2.5 55.8 %exchange.1 = (s32[16,128]{1,0:T(8,128)S(1)}, bf16[4,512,512]{2,1,0:T(8,128)(2,1)S(1)}, bf16[4,16,16,512]{3,2,1,0:T(8,128)(2,1)S(1)}, f32[4,512,512]{2,1,0:T(8,128)S(1)}, f32[4,512,512]{2,1,0:T(8,128)S(1)}) custom-call(s32[1,64]{1,0:T(1,128)S(1)} %bitcast.3, bf16[64,16,512]{2,1,0:T(8,128)(2,1)S(1)} %bitcast.2, f32[4,512,512]{2,1,0:T(8,128)} %lf_hbm.1, ...), custom_call_target="tpu_custom_call" | custom-call | tf_op jit(solution)/shard_map/exchange/pallas_call | solution.py:323
  58.3 5.4 %write_out.1 = (bf16[64,16,512]{2,1,0:T(8,128)(2,1)}, f32[4,512,512]{2,1,0:T(8,128)}, f32[4,512,512]{2,1,0:T(8,128)}) custom-call(s32[16,128]{1,0:T(8,128)S(1)} %get-tuple-element.8.tab_v, bf16[4,512,512]{2,1,0:T(8,128)(2,1)S(1)} %get-tuple-element.9.gath, bf16[4,16,16,512]{3,2,1,0:T(8,128)(2,1)S(1)} %get-tuple-element.10.uall, ...), custom_call_target="tpu_custom_call" | custom-call | tf_op jit(solution)/shard_map/write_out/pallas_call | solution.py:367
Async XLA Ops:
  0.6 1.2 %copy-start = (bf16[1,64,16,512]{3,2,1,0:T(8,128)(2,1)S(1)}, bf16[1,64,16,512]{3,2,1,0:T(8,128)(2,1)}, u32[]{:S(2)}) copy-start(bf16[1,64,16,512]{3,2,1,0:T(8,128)(2,1)} %param.6) | copy-start | bytes 3145732
  1.9 0.7 %copy-start.1 = (s32[64,1]{0,1:T(1,128)S(1)}, s32[64,1]{0,1:T(1,128)}, u32[]{:S(2)}) copy-start(s32[64,1]{0,1:T(1,128)} %param.7) | copy-start | bytes 772

commit v2 on v1

--- a/solution.py
+++ b/solution.py
@@ -12,6 +12,7 @@
 DECAY = 0.9
 EPS = 1e-06
 CHUNKS = 2
+PIECES = 6
 STEPS = (1, 3, 2)
 TAB_ROWS = 16
 ROW_BLOCK, ROW_POS, ROW_OWNER, ROW_START, ROW_COUNT, ROW_PLACE = 0, 1, 2, 3, 4, 5
@@ -60,9 +61,9 @@
 
 
 def exchange(
-    reps, devs, owner_ref, grad_hbm, lf_hbm, rf_hbm, lr_hbm, rr_hbm,
+    reps, devs, owner_hbm, grad_hbm, lf_hbm, rf_hbm, lr_hbm, rr_hbm,
     tab_out, gath, uall, lf_out, rf_out,
-    tab, grad, lroot, rroot, rs_send, rs_recv, stage, half, direct, upd, s_own, s_recv, back,
+    tab, owner, grad, lroot, rroot, rs_send, rs_recv, stage, half, direct, upd, s_own, s_recv, back,
     loc_sem, rs_ss, rs_rs, ag_ss, ag_rs, pr_ss, pr_rs, ot_ss, ot_rs, bk_ss, bk_rs, au_ss, au_rs,
 ):
     r = lax.axis_index("rep")
@@ -72,9 +73,11 @@
     cols = [pl.ds(c * part, part) for c in range(CHUNKS)]
     tile = min(256, width)
     mine = pl.ds(pl.multiple_of(d * rows, rows), rows)
-
-    def rep_peer(k):
-        return (lax.rem(r + k, reps), d)
+    few = places // 2
+    first, last = pl.ds(0, few), pl.ds(few, few)
+
+    def rep_of(k):
+        return lax.rem(r + k, reps)
 
     def dp_peer(t):
         return lax.rem(d + t, devs)
@@ -82,19 +85,15 @@
     def local(src, dst, i):
         return pltpu.make_async_copy(src, dst, loc_sem.at[i])
 
-    loads = [
-        local(grad_hbm, grad, 0),
-        local(lr_hbm, lroot, 1),
-        local(rr_hbm, rroot, 2),
-        local(lf_hbm, lf_out, 3),
-        local(rf_hbm, rf_out, 4),
-    ]
-    for load in loads:
-        load.start()
+    load_owner, load_grad = local(owner_hbm, owner, 0), local(grad_hbm, grad, 1)
+    load_roots = [local(lr_hbm, lroot, 2), local(rr_hbm, rroot, 3)]
+    load_factors = [local(lf_hbm, lf_out, 4), local(rf_hbm, rf_out, 5)]
+    load_owner.start()
+    load_grad.start()
 
     barrier = pltpu.get_barrier_semaphore()
     for k in STEPS:
-        pl.semaphore_signal(barrier, inc=1, device_id=rep_peer(k), device_id_type=MESH)
+        pl.semaphore_signal(barrier, inc=1, device_id=(rep_of(k), d), device_id_type=MESH)
 
     def greet(t, carry):
         pl.semaphore_signal(barrier, inc=1, device_id=(r, dp_peer(t)), device_id_type=MESH)
@@ -102,80 +101,123 @@
 
     lax.fori_loop(1, devs, greet, 0)
 
-    fill_tables(owner_ref, tab_out)
-    to_scalars = local(tab_out, tab, 5)
+    load_owner.wait()
+    fill_tables(owner, tab_out)
+    to_scalars = local(tab_out, tab, 6)
     to_scalars.start()
     to_scalars.wait()
-    loads[0].wait()
-
-    for i, k in enumerate(STEPS):
-        q = lax.rem(r + k, reps)
-
-        def pack(j, carry, i=i, q=q):
-            block = tab[ROW_BLOCK, CAP * j + q]
-            for c in range(CHUNKS):
-                rs_send[c, i, j] = grad[block, :, cols[c]]
+    load_grad.wait()
+
+    def to_rep(piece, src, dst, ss, rs):
+        copy = pltpu.make_async_remote_copy(
+            src_ref=src,
+            dst_ref=dst,
+            send_sem=ss.at[piece],
+            recv_sem=rs.at[piece],
+            device_id=(rep_of(1 if piece % 2 == 0 else reps - 1), d),
+            device_id_type=MESH,
+        )
+        copy.start()
+        return copy
+
+    packing = ((2, 0), (2, few), (1, few), (reps - 1, 0), (1, 0), (reps - 1, few))
+
+    def pack(pieces, c):
+        def step(j, carry):
+            for p in pieces:
+                k, at = packing[p]
+                block = tab[ROW_BLOCK, CAP * (at + j) + rep_of(k)]
+                rows_here = grad[block, :, cols[c]]
+                if p >= 4:
+                    both = rows_here.astype(jnp.float32) + rs_recv[c, p - 4, j].astype(jnp.float32)
+                    rows_here = both.astype(jnp.bfloat16)
+                rs_send[c, p, j] = rows_here
             return carry
 
-        lax.fori_loop(0, places, pack, 0)
-
+        lax.fori_loop(0, few, step, 0)
+
+    def send_sums(p, c):
+        return to_rep(p, rs_send.at[c, p], rs_recv.at[c, p], rs_ss.at[c], rs_rs.at[c])
+
+    for c in range(CHUNKS):
+        pack((0, 1, 2, 3), c)
     pl.semaphore_wait(barrier, reps - 1 + devs - 1)
-
-    def over_rep(src, dst, ss, rs):
-        copies = []
-        for i, k in enumerate(STEPS):
-            copies.append(
-                pltpu.make_async_remote_copy(
-                    src_ref=src(i),
-                    dst_ref=dst(i),
-                    send_sem=ss.at[i],
-                    recv_sem=rs.at[i],
-                    device_id=rep_peer(k),
-                    device_id_type=MESH,
-                )
-            )
-        for copy in copies:
-            copy.start()
-        return copies
-
-    rs = [
-        over_rep(lambda i: rs_send.at[c, i], lambda i: rs_recv.at[c, i], rs_ss.at[c], rs_rs.at[c])
-        for c in range(CHUNKS)
-    ]
+    rs = [[send_sums(p, c) for p in range(4)] for c in range(CHUNKS)]
+    for load in load_roots + load_factors:
+        load.start()
+    for c in range(CHUNKS):
+        for p in (4, 5):
+            rs[c][p - 4].wait_recv()
+            pack((p,), c)
+            rs[c].append(send_sums(p, c))
+
+    def share(buf, ss, rs):
+        return [
+            to_rep(0, buf(0, first), buf(1, first), ss, rs),
+            to_rep(1, buf(0, last), buf(2, last), ss, rs),
+            to_rep(2, buf(0, last), buf(1, last), ss, rs),
+            to_rep(3, buf(0, first), buf(2, first), ss, rs),
+        ]
+
+    def pass_on(copies, buf, ss, rs):
+        copies[0].wait_recv()
+        copies.append(to_rep(4, buf(1, first), buf(3, first), ss, rs))
+        copies[1].wait_recv()
+        copies.append(to_rep(5, buf(2, last), buf(3, last), ss, rs))
+
+    def sums(c):
+        return lambda i, sl: (s_own[c] if i == 0 else s_recv[(i - 1) * CHUNKS + c]).at[sl]
 
     def one(src, dst, ss, rs, to):
         pltpu.make_async_remote_copy(
             src_ref=src, dst_ref=dst, send_sem=ss, recv_sem=rs, device_id=(r, to), device_id_type=MESH
         ).start()
 
+    def to_owners(i, c, q, src, ss, rs):
+        def step(t, carry):
+            o = dp_peer(t)
+            stage[i, o, :, cols[c]] = src[tab[ROW_PLACE + q, o]]
+            one(stage.at[i, o, :, cols[c]], gath.at[i, mine, cols[c]], ss, rs, o)
+            return carry
+
+        lax.fori_loop(1, devs, step, 0)
+        gath[i, mine, cols[c]] = src[tab[ROW_PLACE + q, d]]
+
     ag = []
     for c in range(CHUNKS):
-        for copy in rs[c]:
-            copy.wait_recv()
+        for p in (2, 3, 4, 5):
+            rs[c][p].wait_recv()
 
         def add(j, carry, c=c):
-            block = tab[ROW_BLOCK, CAP * j + r]
-            total = grad[block, :, cols[c]].astype(jnp.float32)
-            for i in range(len(STEPS)):
-                total += rs_recv[c, i, j].astype(jnp.float32)
-            s_own[c][j] = total.astype(jnp.bfloat16)
+            for at, pieces in ((0, (4, 3)), (few, (2, 5))):
+                total = grad[tab[ROW_BLOCK, CAP * (at + j) + r], :, cols[c]].astype(jnp.float32)
+                for p in pieces:
+                    total += rs_recv[c, p, j].astype(jnp.float32)
+                s_own[c][at + j] = total.astype(jnp.bfloat16)
             return carry
 
-        lax.fori_loop(0, places, add, 0)
-
-        def to_owner(t, carry, c=c):
-            o = dp_peer(t)
-            stage[0, o, :, cols[c]] = s_own[c][tab[ROW_PLACE + r, o]]
-            one(stage.at[0, o, :, cols[c]], gath.at[0, mine, cols[c]], pr_ss.at[c], pr_rs.at[c], o)
-            return carry
-
-        lax.fori_loop(1, devs, to_owner, 0)
-        gath[0, mine, cols[c]] = s_own[c][tab[ROW_PLACE + r, d]]
-        ag.append(over_rep(lambda i: s_own[c], lambda i: s_recv[i].at[c], ag_ss.at[c], ag_rs.at[c]))
+        lax.fori_loop(0, few, add, 0)
+        ag.append(share(sums(c), ag_ss.at[c], ag_rs.at[c]))
+        to_owners(0, c, r, s_own[c], pr_ss.at[c], pr_rs.at[c])
+
+    def pass_sums_on(c):
+        pass_on(ag[c], sums(c), ag_ss.at[c], ag_rs.at[c])
+
+    def others(i, c):
+        for p in ((2,), (3,), (4, 5))[i - 1]:
+            ag[c][p].wait_recv()
+        q = rep_of(reps - STEPS[i - 1])
+        to_owners(i, c, q, s_recv[(i - 1) * CHUNKS + c], ot_ss.at[c, i - 1], ot_rs.at[c, i - 1])
+
+    pass_sums_on(0)
+    others(1, 0)
+    others(2, 0)
+    for c in range(1, CHUNKS):
+        pass_sums_on(c)
 
     slot = (r - tab[ROW_START, d]) & 3
-    loads[1].wait()
-    loads[2].wait()
+    for load in load_roots:
+        load.wait()
     for c in range(CHUNKS):
         arrived = gath.at[0, pl.ds(0, rows * (devs - 1)), cols[c]]
         pltpu.make_async_copy(arrived, arrived, pr_rs.at[c]).wait()
@@ -206,23 +248,13 @@
         lax.fori_loop(1, devs, homeward, 0)
         back[c][d] = upd[mine, cols[c]]
 
-    for i, k in enumerate(STEPS):
-        for c in range(CHUNKS):
-            ag[c][i].wait_recv()
-        q = lax.rem(r + reps - k, reps)
-
-        def to_owner_too(t, carry, i=i, q=q):
-            o = dp_peer(t)
-            place = tab[ROW_PLACE + q, o]
-            for c in range(CHUNKS):
-                stage[1 + i, o, :, cols[c]] = s_recv[i][c, place]
-            one(stage.at[1 + i, o], gath.at[1 + i, mine, :], ot_ss.at[i], ot_rs.at[i], o)
-            return carry
-
-        lax.fori_loop(1, devs, to_owner_too, 0)
-        own = tab[ROW_PLACE + q, d]
-        for c in range(CHUNKS):
-            gath[1 + i, mine, cols[c]] = s_recv[i][c, own]
+    others(3, 0)
+    for c in range(1, CHUNKS):
+        for i in (1, 2, 3):
+            others(i, c)
+
+    def steps(c):
+        return lambda i, sl: uall.at[i, sl, :, cols[c]]
 
     au = []
     for c in range(CHUNKS):
@@ -234,32 +266,25 @@
             return carry
 
         lax.fori_loop(0, places, unpack, 0)
-        au.append(
-            over_rep(
-                lambda i: uall.at[0, :, :, cols[c]],
-                lambda i: uall.at[1 + i, :, :, cols[c]],
-                au_ss.at[c],
-                au_rs.at[c],
-            )
-        )
-
-    for c in range(CHUNKS):
-        for copy in rs[c] + ag[c]:
+        au.append(share(steps(c), au_ss.at[c], au_rs.at[c]))
+    for c in range(CHUNKS):
+        pass_on(au[c], steps(c), au_ss.at[c], au_rs.at[c])
+
+    for c in range(CHUNKS):
+        for copy in rs[c] + ag[c] + au[c]:
             copy.wait_send()
-        sent = stage.at[0, pl.ds(0, devs - 1), :, cols[c]]
-        pltpu.make_async_copy(sent, sent, pr_ss.at[c]).wait()
+        for i in range(CAP):
+            sent = stage.at[i, pl.ds(0, devs - 1), :, cols[c]]
+            pltpu.make_async_copy(sent, sent, pr_ss.at[c] if i == 0 else ot_ss.at[c, i - 1]).wait()
+        for i in range(1, CAP):
+            arrived = gath.at[i, pl.ds(0, rows * (devs - 1)), cols[c]]
+            pltpu.make_async_copy(arrived, arrived, ot_rs.at[c, i - 1]).wait()
         sent = back[c].at[pl.ds(0, devs - 1)]
         pltpu.make_async_copy(sent, sent, bk_ss.at[c]).wait()
-    for i in range(len(STEPS)):
-        sent = stage.at[1 + i, pl.ds(0, devs - 1)]
-        pltpu.make_async_copy(sent, sent, ot_ss.at[i]).wait()
-        arrived = gath.at[1 + i, pl.ds(0, rows * (devs - 1)), :]
-        pltpu.make_async_copy(arrived, arrived, ot_rs.at[i]).wait()
-    for copies in au:
-        for copy in copies:
-            copy.wait()
-    loads[3].wait()
-    loads[4].wait()
+        for copy in au[c][2:]:
+            copy.wait_recv()
+    for load in load_factors:
+        load.wait()
 
 
 def write_out(
@@ -317,6 +342,7 @@
     places = blocks // reps
     part = width // CHUNKS
     any_spec = pl.BlockSpec(memory_space=pl.ANY)
+    hbm_spec = pl.BlockSpec(memory_space=pltpu.HBM)
     vmem_spec = pl.BlockSpec(memory_space=pltpu.VMEM)
     dma = pltpu.SemaphoreType.DMA
     three = len(STEPS)
@@ -330,35 +356,36 @@
             in_vmem((CAP, width, width), f32),
             in_vmem((CAP, width, width), f32),
         ],
-        in_specs=[vmem_spec] + [any_spec] * 5,
+        in_specs=[hbm_spec] * 6,
         out_specs=[vmem_spec] * 5,
         scratch_shapes=[
             pltpu.SMEM((TAB_ROWS, 128), jnp.int32),
+            pltpu.VMEM((1, blocks), jnp.int32),
             pltpu.VMEM((blocks, rows, width), bf16),
             pltpu.VMEM((CAP, width, width), bf16),
             pltpu.VMEM((CAP, width, width), bf16),
-            pltpu.VMEM((CHUNKS, three, places, rows, part), bf16),
-            pltpu.VMEM((CHUNKS, three, places, rows, part), bf16),
+            pltpu.VMEM((CHUNKS, PIECES, places // 2, rows, part), bf16),
+            pltpu.VMEM((CHUNKS, PIECES, places // 2, rows, part), bf16),
             pltpu.VMEM((CAP, devs, rows, width), bf16),
             pltpu.VMEM((width, width), bf16),
             pltpu.VMEM((width, width), f32),
             pltpu.VMEM((width, width), bf16),
             [pltpu.VMEM((places, rows, part), bf16)] * CHUNKS,
-            [pltpu.VMEM((CHUNKS, places, rows, part), bf16)] * three,
+            [pltpu.VMEM((places, rows, part), bf16)] * (CHUNKS * three),
             [pltpu.VMEM((devs, rows, part), bf16)] * CHUNKS,
-            dma((6,)),
-            dma((CHUNKS, three)),
-            dma((CHUNKS, three)),
+            dma((7,)),
+            dma((CHUNKS, PIECES)),
+            dma((CHUNKS, PIECES)),
+            dma((CHUNKS, PIECES)),
+            dma((CHUNKS, PIECES)),
+            dma((CHUNKS,)),
+            dma((CHUNKS,)),
             dma((CHUNKS, three)),
             dma((CHUNKS, three)),
             dma((CHUNKS,)),
             dma((CHUNKS,)),
-            dma((three,)),
-            dma((three,)),
-            dma((CHUNKS,)),
-            dma((CHUNKS,)),
-            dma((CHUNKS, three)),
-            dma((CHUNKS, three)),
+            dma((CHUNKS, PIECES)),
+            dma((CHUNKS, PIECES)),
         ],
         compiler_params=pltpu.CompilerParams(
             collective_id=0, has_side_effects=True, vmem_limit_bytes=40 * 2**20
@@ -373,7 +400,7 @@
             jax.ShapeDtypeStruct((CAP, width, width), f32),
         ],
         in_specs=[any_spec] + [vmem_spec] * 4,
-        out_specs=[pl.BlockSpec(memory_space=pltpu.HBM)] * 3,
+        out_specs=[hbm_spec] * 3,
         scratch_shapes=[
             pltpu.SMEM((TAB_ROWS, 128), jnp.int32),
             pltpu.VMEM((CAP, width, width), f32),

time: 63.9 us -> 58.4 us (0.914)
  Pallas kernels: 61.2 us -> 55.7 us
    pallas_call x1, Pallas kernels: 55.8 us -> 50.3 us  [shards(): pl.pallas_call(functools.partial(exchange, reps, devs), name='exchange',...]
where the time goes in v2:
time: 58.4 us; the launch traced here: 58.2 us
  Pallas kernels  55.7 us (95%)
  local copies, waits for them, and re-layouts  1.87 us (3%)
  between operations  0.65 us (1%)
    pallas_call x1, Pallas kernels, shards(): pl.pallas_call(functools.partial(exchange, reps, devs), name='exchange',...  50.3 us
    pallas_call x1, Pallas kernels, shards(): pl.pallas_call(functools.partial(write_out, reps), name='write_out', out_...  5.41 us
    unnamed x4, local copies, waits for them, and re-layouts  1.87 us

profile of v2, /device:TPU:1, one launch (start us, length us, event | category | flops | bytes accessed | tf_op | source)
XLA Modules:
  0.0 58.2 jit_solution(9457872309296130998)
XLA Ops:
  0.6 0.0 copy-start
  0.6 1.2 %copy-done = bf16[1,64,16,512]{3,2,1,0:T(8,128)(2,1)S(1)} copy-done((bf16[1,64,16,512]{3,2,1,0:T(8,128)(2,1)S(1)}, bf16[1,64,16,512]{3,2,1,0:T(8,128)(2,1)}, u32[]{:S(2)}) %copy-start) | copy-done | bytes 1048600
  1.9 0.0 copy-start.1
  1.9 0.7 %copy-done.1 = s32[64,1]{0,1:T(1,128)S(1)} copy-done((s32[64,1]{0,1:T(1,128)S(1)}, s32[64,1]{0,1:T(1,128)}, u32[]{:S(2)}) %copy-start.1) | copy-done | bytes 280
  2.5 50.3 %exchange.1 = (s32[16,128]{1,0:T(8,128)S(1)}, bf16[4,512,512]{2,1,0:T(8,128)(2,1)S(1)}, bf16[4,16,16,512]{3,2,1,0:T(8,128)(2,1)S(1)}, f32[4,512,512]{2,1,0:T(8,128)S(1)}, f32[4,512,512]{2,1,0:T(8,128)S(1)}) custom-call(s32[1,64]{1,0:T(1,128)S(1)} %bitcast.3, bf16[64,16,512]{2,1,0:T(8,128)(2,1)S(1)} %bitcast.2, f32[4,512,512]{2,1,0:T(8,128)} %lf_hbm.1, ...), custom_call_target="tpu_custom_call" | custom-call | tf_op jit(solution)/shard_map/exchange/pallas_call | solution.py:349
  52.8 5.4 %write_out.1 = (bf16[64,16,512]{2,1,0:T(8,128)(2,1)}, f32[4,512,512]{2,1,0:T(8,128)}, f32[4,512,512]{2,1,0:T(8,128)}) custom-call(s32[16,128]{1,0:T(8,128)S(1)} %get-tuple-element.8.tab_v, bf16[4,512,512]{2,1,0:T(8,128)(2,1)S(1)} %get-tuple-element.9.gath, bf16[4,16,16,512]{3,2,1,0:T(8,128)(2,1)S(1)} %get-tuple-element.10.uall, ...), custom_call_target="tpu_custom_call" | custom-call | tf_op jit(solution)/shard_map/write_out/pallas_call | solution.py:394
Async XLA Ops:
  0.6 1.2 %copy-start = (bf16[1,64,16,512]{3,2,1,0:T(8,128)(2,1)S(1)}, bf16[1,64,16,512]{3,2,1,0:T(8,128)(2,1)}, u32[]{:S(2)}) copy-start(bf16[1,64,16,512]{3,2,1,0:T(8,128)(2,1)} %param.6) | copy-start | bytes 3145732
  1.9 0.7 %copy-start.1 = (s32[64,1]{0,1:T(1,128)S(1)}, s32[64,1]{0,1:T(1,128)}, u32[]{:S(2)}) copy-start(s32[64,1]{0,1:T(1,128)} %param.7) | copy-start | bytes 772

commit v3 on v2

--- a/solution.py
+++ b/solution.py
@@ -18,8 +18,18 @@
 ROW_BLOCK, ROW_POS, ROW_OWNER, ROW_START, ROW_COUNT, ROW_PLACE = 0, 1, 2, 3, 4, 5
 
 
+def far_order():
+    near = {0: 0, 1: 1, 2: 2, 3: 1}
+    every = [(z, x, c) for z in range(4) for x in range(4) for c in range(2) if (z, x, c) != (0, 0, 0)]
+    return sorted(every, key=lambda p: -(near[p[0]] + near[p[1]]))
+
+
 def in_vmem(shape, dtype):
     return pltpu.VMEM(shape, dtype)
+
+
+def in_hbm(x):
+    return pltpu.with_memory_space_constraint(x, pltpu.HBM)
 
 
 def from_vmem(x):
@@ -62,9 +72,9 @@
 
 def exchange(
     reps, devs, owner_hbm, grad_hbm, lf_hbm, rf_hbm, lr_hbm, rr_hbm,
-    tab_out, gath, uall, lf_out, rf_out,
-    tab, owner, grad, lroot, rroot, rs_send, rs_recv, stage, half, direct, upd, s_own, s_recv, back,
-    loc_sem, rs_ss, rs_rs, ag_ss, ag_rs, pr_ss, pr_rs, ot_ss, ot_rs, bk_ss, bk_rs, au_ss, au_rs,
+    tab_out, left_gram, right_gram, uall, lf_out, rf_out,
+    tab, gath, owner, grad, lroot, rroot, rs_send, rs_recv, stage, half, direct, upd, s_own, s_recv, back,
+    loc_sem, rs_ss, rs_rs, ag_ss, ag_rs, pr_ss, pr_rs, ot_ss, ot_rs, ow_ss, ow_rs, bk_ss, bk_rs, au_ss, au_rs,
 ):
     r = lax.axis_index("rep")
     d = lax.axis_index("dp")
@@ -80,12 +90,16 @@
         return lax.rem(r + k, reps)
 
     def dp_peer(t):
-        return lax.rem(d + t, devs)
+        if not isinstance(t, tuple):
+            return lax.rem(d + t, devs)
+        dz, dx, dc = t
+        z, x, c = d // 8, lax.rem(d // 2, 4), lax.rem(d, 2)
+        return lax.rem(z + dz, 4) * 8 + lax.rem(x + dx, 4) * 2 + lax.rem(c + dc, 2)
 
     def local(src, dst, i):
         return pltpu.make_async_copy(src, dst, loc_sem.at[i])
 
-    load_owner, load_grad = local(owner_hbm, owner, 0), local(grad_hbm, grad, 1)
+    load_owner, load_grad = local(owner_hbm, owner, 0), local(grad_hbm.at[0], grad, 1)
     load_roots = [local(lr_hbm, lroot, 2), local(rr_hbm, rroot, 3)]
     load_factors = [local(lf_hbm, lf_out, 4), local(rf_hbm, rf_out, 5)]
     load_owner.start()
@@ -151,19 +165,15 @@
             pack((p,), c)
             rs[c].append(send_sums(p, c))
 
-    def share(buf, ss, rs):
-        return [
-            to_rep(0, buf(0, first), buf(1, first), ss, rs),
-            to_rep(1, buf(0, last), buf(2, last), ss, rs),
-            to_rep(2, buf(0, last), buf(1, last), ss, rs),
-            to_rep(3, buf(0, first), buf(2, first), ss, rs),
-        ]
+    def share(pieces, buf, ss, rs):
+        halves = (first, last, last, first)
+        return {p: to_rep(p, buf(0, halves[p]), buf(1 + p % 2, halves[p]), ss, rs) for p in pieces}
 
     def pass_on(copies, buf, ss, rs):
         copies[0].wait_recv()
-        copies.append(to_rep(4, buf(1, first), buf(3, first), ss, rs))
+        copies[4] = to_rep(4, buf(1, first), buf(3, first), ss, rs)
         copies[1].wait_recv()
-        copies.append(to_rep(5, buf(2, last), buf(3, last), ss, rs))
+        copies[5] = to_rep(5, buf(2, last), buf(3, last), ss, rs)
 
     def sums(c):
         return lambda i, sl: (s_own[c] if i == 0 else s_recv[(i - 1) * CHUNKS + c]).at[sl]
@@ -180,7 +190,8 @@
             one(stage.at[i, o, :, cols[c]], gath.at[i, mine, cols[c]], ss, rs, o)
             return carry
 
-        lax.fori_loop(1, devs, step, 0)
+        for p in far_order():
+            step(p, 0)
         gath[i, mine, cols[c]] = src[tab[ROW_PLACE + q, d]]
 
     ag = []
@@ -197,7 +208,7 @@
             return carry
 
         lax.fori_loop(0, few, add, 0)
-        ag.append(share(sums(c), ag_ss.at[c], ag_rs.at[c]))
+        ag.append(share((0, 1, 2 + c % 2), sums(c), ag_ss.at[c], ag_rs.at[c]))
         to_owners(0, c, r, s_own[c], pr_ss.at[c], pr_rs.at[c])
 
     def pass_sums_on(c):
@@ -209,18 +220,23 @@
         q = rep_of(reps - STEPS[i - 1])
         to_owners(i, c, q, s_recv[(i - 1) * CHUNKS + c], ot_ss.at[c, i - 1], ot_rs.at[c, i - 1])
 
+    def from_neighbour(i, c):
+        arrived = gath.at[0, :, cols[c]]
+        return to_rep(i, arrived, gath.at[1 + i, :, cols[c]], ow_ss.at[c], ow_rs.at[c])
+
     pass_sums_on(0)
     others(1, 0)
-    others(2, 0)
     for c in range(1, CHUNKS):
         pass_sums_on(c)
 
     slot = (r - tab[ROW_START, d]) & 3
     for load in load_roots:
         load.wait()
+    ow = []
     for c in range(CHUNKS):
         arrived = gath.at[0, pl.ds(0, rows * (devs - 1)), cols[c]]
         pltpu.make_async_copy(arrived, arrived, pr_rs.at[c]).wait()
+        ow.append(from_neighbour(1 - c % 2, c))
         for m in range(0, width, tile):
             half[m : m + tile, cols[c]] = jnp.dot(
                 lroot[slot, m : m + tile, :], gath[0, :, cols[c]], preferred_element_type=jnp.float32
@@ -245,13 +261,33 @@
             one(upd.at[theirs, cols[c]], back[c].at[d], bk_ss.at[c], bk_rs.at[c], to)
             return carry
 
-        lax.fori_loop(1, devs, homeward, 0)
+        for p in far_order():
+            homeward(p, 0)
         back[c][d] = upd[mine, cols[c]]
 
     others(3, 0)
     for c in range(1, CHUNKS):
-        for i in (1, 2, 3):
-            others(i, c)
+        others(1 + c % 2, c)
+        others(3, c)
+
+    def gram(i):
+        if i > 0:
+            for c in range(CHUNKS):
+                if i == 3 or i == 1 + c % 2:
+                    arrived = gath.at[i, pl.ds(0, rows * (devs - 1)), cols[c]]
+                    pltpu.make_async_copy(arrived, arrived, ot_rs.at[c, i - 1]).wait()
+                else:
+                    ow[c].wait_recv()
+        for m in range(0, width, tile):
+            sl = pl.ds(m, tile)
+            left_gram[i, sl, :] = lax.dot_general(
+                gath[i, sl, :], gath[i], (((1,), (1,)), ((), ())), preferred_element_type=jnp.float32
+            )
+            right_gram[i, sl, :] = lax.dot_general(
+                gath[i, :, sl], gath[i], (((0,), (0,)), ((), ())), preferred_element_type=jnp.float32
+            )
+
+    gram(0)
 
     def steps(c):
         return lambda i, sl: uall.at[i, sl, :, cols[c]]
@@ -266,35 +302,35 @@
             return carry
 
         lax.fori_loop(0, places, unpack, 0)
-        au.append(share(steps(c), au_ss.at[c], au_rs.at[c]))
+        au.append(share((0, 1, 2, 3), steps(c), au_ss.at[c], au_rs.at[c]))
+    gram(1)
     for c in range(CHUNKS):
         pass_on(au[c], steps(c), au_ss.at[c], au_rs.at[c])
 
-    for c in range(CHUNKS):
-        for copy in rs[c] + ag[c] + au[c]:
+    gram(2)
+    gram(3)
+
+    for c in range(CHUNKS):
+        for copy in rs[c] + list(ag[c].values()) + list(au[c].values()) + [ow[c]]:
             copy.wait_send()
-        for i in range(CAP):
+        for i in (0, 1 + c % 2, 3):
             sent = stage.at[i, pl.ds(0, devs - 1), :, cols[c]]
             pltpu.make_async_copy(sent, sent, pr_ss.at[c] if i == 0 else ot_ss.at[c, i - 1]).wait()
-        for i in range(1, CAP):
-            arrived = gath.at[i, pl.ds(0, rows * (devs - 1)), cols[c]]
-            pltpu.make_async_copy(arrived, arrived, ot_rs.at[c, i - 1]).wait()
         sent = back[c].at[pl.ds(0, devs - 1)]
         pltpu.make_async_copy(sent, sent, bk_ss.at[c]).wait()
-        for copy in au[c][2:]:
-            copy.wait_recv()
+        for p in (2, 3, 4, 5):
+            au[c][p].wait_recv()
     for load in load_factors:
         load.wait()
 
 
 def write_out(
-    reps, tab_v, gath, uall, lf, rf, update, left_out, right_out, tab, left_buf, right_buf, sems
+    reps, tab_v, left_gram, right_gram, uall, lf, rf, update, left_out, right_out, tab, left_buf, right_buf, sems
 ):
     r = lax.axis_index("rep")
     d = lax.axis_index("dp")
-    blocks, width = update.shape[0], gath.shape[2]
-    places = uall.shape[1]
-    tile = min(256, width)
+    blocks, width = update.shape[0], lf.shape[2]
+    tile = min(128, width)
     load = pltpu.make_async_copy(tab_v, tab, sems.at[0])
     load.start()
     load.wait()
@@ -302,6 +338,18 @@
     def buffer_of(q):
         step = lax.rem(r - q + reps, reps)
         return jnp.where(step < 2, step, 5 - step)
+
+    start, count = tab[ROW_START, d], tab[ROW_COUNT, d]
+    weight = (1.0 - DECAY) / width
+    sides = ((lf, left_gram, left_buf, left_out), (rf, right_gram, right_buf, right_out))
+    for s in range(CAP):
+        valid = s < count
+        i = buffer_of((start + s) & 3)
+        for factor, gram, buf, out in sides:
+            for m in range(0, width, tile):
+                sl = pl.ds(m, tile)
+                buf[s, sl, :] = DECAY * factor[s, sl, :] + jnp.where(valid, weight * gram[i, sl, :], 0.0)
+                pltpu.make_async_copy(buf.at[s, sl], out.at[s, sl], sems.at[2]).start()
 
     def put(b, carry):
         pos = tab[ROW_POS, b]
@@ -309,31 +357,9 @@
         return carry
 
     lax.fori_loop(0, blocks, put, 0)
-    start, count = tab[ROW_START, d], tab[ROW_COUNT, d]
-    weight = (1.0 - DECAY) / width
-    copies = []
-    for s in range(CAP):
-        valid = s < count
-        idx = buffer_of((start + s) & 3)
-        for side, (factor, buf, out) in enumerate(((lf, left_buf, left_out), (rf, right_buf, right_out))):
-            for m in range(0, width, tile):
-                sl = pl.ds(m, tile)
-                if side == 0:
-                    gram = lax.dot_general(
-                        gath[idx, sl, :], gath[idx], (((1,), (1,)), ((), ())), preferred_element_type=jnp.float32
-                    )
-                else:
-                    gram = lax.dot_general(
-                        gath[idx, :, sl], gath[idx], (((0,), (0,)), ((), ())), preferred_element_type=jnp.float32
-                    )
-                buf[s, sl, :] = DECAY * factor[s, sl, :] + jnp.where(valid, weight * gram, 0.0)
-                copy = pltpu.make_async_copy(buf.at[s, sl], out.at[s, sl], sems.at[2])
-                copy.start()
-                copies.append(copy)
     pltpu.make_async_copy(left_buf, left_out, sems.at[2]).wait()
     pltpu.make_async_copy(right_buf, right_out, sems.at[2]).wait()
-    flat = uall
-    pltpu.make_async_copy(flat, flat, sems.at[1]).wait()
+    pltpu.make_async_copy(uall, uall, sems.at[1]).wait()
 
 
 def shards(reps, devs, gradient, owner, left_factor, right_factor, left_root, right_root):
@@ -346,20 +372,22 @@
     vmem_spec = pl.BlockSpec(memory_space=pltpu.VMEM)
     dma = pltpu.SemaphoreType.DMA
     three = len(STEPS)
-    tab, gath, uall, lf, rf = pl.pallas_call(
+    tab, left_gram, right_gram, uall, lf, rf = pl.pallas_call(
         functools.partial(exchange, reps, devs),
         name="exchange",
         out_shape=[
             in_vmem((TAB_ROWS, 128), jnp.int32),
-            in_vmem((CAP, width, width), bf16),
+            in_vmem((CAP, width, width), f32),
+            in_vmem((CAP, width, width), f32),
             in_vmem((CAP, places, rows, width), bf16),
             in_vmem((CAP, width, width), f32),
             in_vmem((CAP, width, width), f32),
         ],
         in_specs=[hbm_spec] * 6,
-        out_specs=[vmem_spec] * 5,
+        out_specs=[vmem_spec] * 6,
         scratch_shapes=[
             pltpu.SMEM((TAB_ROWS, 128), jnp.int32),
+            pltpu.VMEM((CAP, width, width), bf16),
             pltpu.VMEM((1, blocks), jnp.int32),
             pltpu.VMEM((blocks, rows, width), bf16),
             pltpu.VMEM((CAP, width, width), bf16),
@@ -382,6 +410,8 @@
             dma((CHUNKS,)),
             dma((CHUNKS, three)),
             dma((CHUNKS, three)),
+            dma((CHUNKS, PIECES)),
+            dma((CHUNKS, PIECES)),
             dma((CHUNKS,)),
             dma((CHUNKS,)),
             dma((CHUNKS, PIECES)),
@@ -390,7 +420,7 @@
         compiler_params=pltpu.CompilerParams(
             collective_id=0, has_side_effects=True, vmem_limit_bytes=40 * 2**20
         ),
-    )(owner.reshape(1, blocks), gradient[0], left_factor, right_factor, left_root, right_root)
+    )(in_hbm(owner.reshape(1, blocks)), *(in_hbm(x) for x in (gradient, left_factor, right_factor, left_root, right_root)))
     update, left_out, right_out = pl.pallas_call(
         functools.partial(write_out, reps),
         name="write_out",
@@ -399,7 +429,7 @@
             jax.ShapeDtypeStruct((CAP, width, width), f32),
             jax.ShapeDtypeStruct((CAP, width, width), f32),
         ],
-        in_specs=[any_spec] + [vmem_spec] * 4,
+        in_specs=[any_spec] + [vmem_spec] * 5,
         out_specs=[hbm_spec] * 3,
         scratch_shapes=[
             pltpu.SMEM((TAB_ROWS, 128), jnp.int32),
@@ -408,7 +438,7 @@
             dma((3,)),
         ],
         compiler_params=pltpu.CompilerParams(vmem_limit_bytes=24 * 2**20),
-    )(tab, *(from_vmem(x) for x in (gath, uall, lf, rf)))
+    )(tab, *(from_vmem(x) for x in (left_gram, right_gram, uall, lf, rf)))
     return update, left_out, right_out
 
 

time: 58.4 us -> 53.2 us (0.911)
  Pallas kernels: 55.7 us -> 52.4 us
  local copies, waits for them, and re-layouts: 1.87 us -> 0 us
    pallas_call x1, Pallas kernels: 50.3 us -> 48.1 us  [shards(): pl.pallas_call(functools.partial(exchange, reps, devs), name='exchange',...]
    unnamed x4 -> x0, local copies, waits for them, and re-layouts: 1.87 us -> none
    pallas_call x1, Pallas kernels: 5.41 us -> 4.28 us  [shards(): pl.pallas_call(functools.partial(write_out, reps), name='write_out', out_...]
where the time goes in v3:
time: 53.2 us; the launch traced here: 53 us
  Pallas kernels  52.4 us (98%)
  between operations  0.64 us (1%)
    pallas_call x1, Pallas kernels, shards(): pl.pallas_call(functools.partial(exchange, reps, devs), name='exchange',...  48.1 us
    pallas_call x1, Pallas kernels, shards(): pl.pallas_call(functools.partial(write_out, reps), name='write_out', out_...  4.28 us

profile of v3, /device:TPU:1, one launch (start us, length us, event | category | flops | bytes accessed | tf_op | source)
XLA Modules:
  0.0 53.0 jit_solution(8017395816210964638)
XLA Ops:
  0.6 48.1 %exchange.1 = (s32[16,128]{1,0:T(8,128)S(1)}, f32[4,512,512]{2,1,0:T(8,128)S(1)}, f32[4,512,512]{2,1,0:T(8,128)S(1)}, bf16[4,16,16,512]{3,2,1,0:T(8,128)(2,1)S(1...) custom-call(s32[1,64]{1,0:T(1,128)} %bitcast.1, bf16[1,64,16,512]{3,2,1,0:T(8,128)(2,1)} %grad_hbm.1, ...), custom_call_target="tpu_custom_call" | custom-call | tf_op jit(solution)/shard_map/exchange/pallas_call | solution.py:375
  48.8 4.3 %write_out.1 = (bf16[64,16,512]{2,1,0:T(8,128)(2,1)}, f32[4,512,512]{2,1,0:T(8,128)}, f32[4,512,512]{2,1,0:T(8,128)}) custom-call(s32[16,128]{1,0:T(8,128)S(1)} %get-tuple-element.9.tab_v, f32[4,512,512]{2,1,0:T(8,128)S(1)} %get-tuple-element.10.left_gram, f32[4,512,512]{2,1,0:T(8,128)S(1)} %get-tuple-element.11.right_gram, ...), custom_call_target="tpu_custom_call" | custom-call | tf_op jit(solution)/shard_map/write_out/pallas_call | solution.py:424

commit v4 on v3

--- a/solution.py
+++ b/solution.py
@@ -113,7 +113,8 @@
         pl.semaphore_signal(barrier, inc=1, device_id=(r, dp_peer(t)), device_id_type=MESH)
         return carry
 
-    lax.fori_loop(1, devs, greet, 0)
+    for p in far_order():
+        greet(p, 0)
 
     load_owner.wait()
     fill_tables(owner, tab_out)
@@ -148,7 +149,7 @@
                 rs_send[c, p, j] = rows_here
             return carry
 
-        lax.fori_loop(0, few, step, 0)
+        lax.fori_loop(0, few, step, 0, unroll=True)
 
     def send_sums(p, c):
         return to_rep(p, rs_send.at[c, p], rs_recv.at[c, p], rs_ss.at[c], rs_rs.at[c])
@@ -156,14 +157,18 @@
     for c in range(CHUNKS):
         pack((0, 1, 2, 3), c)
     pl.semaphore_wait(barrier, reps - 1 + devs - 1)
-    rs = [[send_sums(p, c) for p in range(4)] for c in range(CHUNKS)]
+    rs = [{p: send_sums(p, c) for p in (range(4) if c == 0 else range(2))} for c in range(CHUNKS)]
     for load in load_roots + load_factors:
         load.start()
     for c in range(CHUNKS):
         for p in (4, 5):
             rs[c][p - 4].wait_recv()
             pack((p,), c)
-            rs[c].append(send_sums(p, c))
+            rs[c][p] = send_sums(p, c)
+        if c == 0:
+            for e in range(1, CHUNKS):
+                for p in (2, 3):
+                    rs[e][p] = send_sums(p, e)
 
     def share(pieces, buf, ss, rs):
         halves = (first, last, last, first)
@@ -207,9 +212,11 @@
                 s_own[c][at + j] = total.astype(jnp.bfloat16)
             return carry
 
-        lax.fori_loop(0, few, add, 0)
-        ag.append(share((0, 1, 2 + c % 2), sums(c), ag_ss.at[c], ag_rs.at[c]))
+        lax.fori_loop(0, few, add, 0, unroll=True)
+        ag.append(share((0, 1, 2 + c % 2), sums(c), ag_ss.at[c], ag_rs.at[c]) if c == 0 else {})
         to_owners(0, c, r, s_own[c], pr_ss.at[c], pr_rs.at[c])
+        if c > 0:
+            ag[c] = share((0, 1, 2 + c % 2), sums(c), ag_ss.at[c], ag_rs.at[c])
 
     def pass_sums_on(c):
         pass_on(ag[c], sums(c), ag_ss.at[c], ag_rs.at[c])
@@ -301,17 +308,19 @@
             uall[0, j, :, cols[c]] = back[c][tab[ROW_OWNER, CAP * j + r]]
             return carry
 
-        lax.fori_loop(0, places, unpack, 0)
-        au.append(share((0, 1, 2, 3), steps(c), au_ss.at[c], au_rs.at[c]))
+        lax.fori_loop(0, places, unpack, 0, unroll=True)
+        au.append(share((0, 1, 2, 3) if c == 0 else (0, 1), steps(c), au_ss.at[c], au_rs.at[c]))
+    for c in range(CHUNKS):
+        if c > 0:
+            au[c].update(share((2, 3), steps(c), au_ss.at[c], au_rs.at[c]))
+        pass_on(au[c], steps(c), au_ss.at[c], au_rs.at[c])
+
     gram(1)
-    for c in range(CHUNKS):
-        pass_on(au[c], steps(c), au_ss.at[c], au_rs.at[c])
-
     gram(2)
     gram(3)
 
     for c in range(CHUNKS):
-        for copy in rs[c] + list(ag[c].values()) + list(au[c].values()) + [ow[c]]:
+        for copy in list(rs[c].values()) + list(ag[c].values()) + list(au[c].values()) + [ow[c]]:
             copy.wait_send()
         for i in (0, 1 + c % 2, 3):
             sent = stage.at[i, pl.ds(0, devs - 1), :, cols[c]]

time: 53.2 us -> 51 us (0.959)
  Pallas kernels: 52.4 us -> 50.2 us
    pallas_call x1, Pallas kernels: 48.1 us -> 45.9 us  [shards(): pl.pallas_call(functools.partial(exchange, reps, devs), name='exchange',...]
where the time goes in v4:
time: 51 us; the launch traced here: 50.9 us
  Pallas kernels  50.2 us (98%)
  between operations  0.64 us (1%)
    pallas_call x1, Pallas kernels, shards(): pl.pallas_call(functools.partial(exchange, reps, devs), name='exchange',...  45.9 us
    pallas_call x1, Pallas kernels, shards(): pl.pallas_call(functools.partial(write_out, reps), name='write_out', out_...  4.28 us

profile of v4, /device:TPU:1, one launch (start us, length us, event | category | flops | bytes accessed | tf_op | source)
XLA Modules:
  0.0 50.9 jit_solution(890791125189856520)
XLA Ops:
  0.6 45.9 %exchange.1 = (s32[16,128]{1,0:T(8,128)S(1)}, f32[4,512,512]{2,1,0:T(8,128)S(1)}, f32[4,512,512]{2,1,0:T(8,128)S(1)}, bf16[4,16,16,512]{3,2,1,0:T(8,128)(2,1)S(1...) custom-call(s32[1,64]{1,0:T(1,128)} %bitcast.1, bf16[1,64,16,512]{3,2,1,0:T(8,128)(2,1)} %grad_hbm.1, ...), custom_call_target="tpu_custom_call" | custom-call | tf_op jit(solution)/shard_map/exchange/pallas_call | solution.py:384
  46.6 4.3 %write_out.1 = (bf16[64,16,512]{2,1,0:T(8,128)(2,1)}, f32[4,512,512]{2,1,0:T(8,128)}, f32[4,512,512]{2,1,0:T(8,128)}) custom-call(s32[16,128]{1,0:T(8,128)S(1)} %get-tuple-element.9.tab_v, f32[4,512,512]{2,1,0:T(8,128)S(1)} %get-tuple-element.10.left_gram, f32[4,512,512]{2,1,0:T(8,128)S(1)} %get-tuple-element.11.right_gram, ...), custom_call_target="tpu_custom_call" | custom-call | tf_op jit(solution)/shard_map/write_out/pallas_call | solution.py:433

commit v5 on v4

--- a/solution.py
+++ b/solution.py
@@ -12,6 +12,7 @@
 DECAY = 0.9
 EPS = 1e-06
 CHUNKS = 2
+BACK = (0, 256, 512)
 PIECES = 6
 STEPS = (1, 3, 2)
 TAB_ROWS = 16
@@ -81,6 +82,7 @@
     places, rows, width = s_own[0].shape[0], grad.shape[1], grad.shape[2]
     part = width // CHUNKS
     cols = [pl.ds(c * part, part) for c in range(CHUNKS)]
+    bcols = [pl.ds(b * width // BACK[-1], (e - b) * width // BACK[-1]) for b, e in zip(BACK, BACK[1:])]
     tile = min(256, width)
     mine = pl.ds(pl.multiple_of(d * rows, rows), rows)
     few = places // 2
@@ -260,21 +262,22 @@
     for m in range(0, width, tile):
         upd[m : m + tile, :] = (direct[m : m + tile, :] * scale).astype(jnp.bfloat16)
 
-    for c in range(CHUNKS):
+    for c in range(len(bcols)):
 
         def homeward(t, carry, c=c):
             to = dp_peer(t)
             theirs = pl.ds(pl.multiple_of(to * rows, rows), rows)
-            one(upd.at[theirs, cols[c]], back[c].at[d], bk_ss.at[c], bk_rs.at[c], to)
+            one(upd.at[theirs, bcols[c]], back[c].at[d], bk_ss.at[c], bk_rs.at[c], to)
             return carry
 
         for p in far_order():
             homeward(p, 0)
-        back[c][d] = upd[mine, cols[c]]
-
+        back[c][d] = upd[mine, bcols[c]]
+
+    for c in range(1, CHUNKS):
+        others(1 + c % 2, c)
     others(3, 0)
     for c in range(1, CHUNKS):
-        others(1 + c % 2, c)
         others(3, c)
 
     def gram(i):
@@ -296,35 +299,38 @@
 
     gram(0)
 
+    gram(1)
+
     def steps(c):
-        return lambda i, sl: uall.at[i, sl, :, cols[c]]
+        return lambda i, sl: uall.at[i, sl, :, bcols[c]]
 
     au = []
-    for c in range(CHUNKS):
+    for c in range(len(bcols)):
         arrived = back[c].at[pl.ds(0, devs - 1)]
         pltpu.make_async_copy(arrived, arrived, bk_rs.at[c]).wait()
 
         def unpack(j, carry, c=c):
-            uall[0, j, :, cols[c]] = back[c][tab[ROW_OWNER, CAP * j + r]]
+            uall[0, j, :, bcols[c]] = back[c][tab[ROW_OWNER, CAP * j + r]]
             return carry
 
         lax.fori_loop(0, places, unpack, 0, unroll=True)
-        au.append(share((0, 1, 2, 3) if c == 0 else (0, 1), steps(c), au_ss.at[c], au_rs.at[c]))
-    for c in range(CHUNKS):
+        au.append(share((0, 1), steps(c), au_ss.at[c], au_rs.at[c]))
         if c > 0:
-            au[c].update(share((2, 3), steps(c), au_ss.at[c], au_rs.at[c]))
-        pass_on(au[c], steps(c), au_ss.at[c], au_rs.at[c])
-
-    gram(1)
+            pass_on(au[c - 1], steps(c - 1), au_ss.at[c - 1], au_rs.at[c - 1])
+        au[c].update(share((2, 3), steps(c), au_ss.at[c], au_rs.at[c]))
+    pass_on(au[-1], steps(len(bcols) - 1), au_ss.at[len(bcols) - 1], au_rs.at[len(bcols) - 1])
     gram(2)
     gram(3)
 
     for c in range(CHUNKS):
-        for copy in list(rs[c].values()) + list(ag[c].values()) + list(au[c].values()) + [ow[c]]:
+        for copy in list(rs[c].values()) + list(ag[c].values()) + [ow[c]]:
             copy.wait_send()
         for i in (0, 1 + c % 2, 3):
             sent = stage.at[i, pl.ds(0, devs - 1), :, cols[c]]
             pltpu.make_async_copy(sent, sent, pr_ss.at[c] if i == 0 else ot_ss.at[c, i - 1]).wait()
+    for c in range(len(bcols)):
+        for copy in au[c].values():
+            copy.wait_send()
         sent = back[c].at[pl.ds(0, devs - 1)]
         pltpu.make_async_copy(sent, sent, bk_ss.at[c]).wait()
         for p in (2, 3, 4, 5):
@@ -339,16 +345,20 @@
     r = lax.axis_index("rep")
     d = lax.axis_index("dp")
     blocks, width = update.shape[0], lf.shape[2]
-    tile = min(128, width)
+    tile = min(64, width)
     load = pltpu.make_async_copy(tab_v, tab, sems.at[0])
     load.start()
-    load.wait()
 
     def buffer_of(q):
         step = lax.rem(r - q + reps, reps)
         return jnp.where(step < 2, step, 5 - step)
 
-    start, count = tab[ROW_START, d], tab[ROW_COUNT, d]
+    def mine(row):
+        values = tab_v[row : row + 1, :]
+        lane = lax.broadcasted_iota(jnp.int32, values.shape, 1)
+        return jnp.sum(jnp.where(lane == d, values, 0))
+
+    start, count = mine(ROW_START), mine(ROW_COUNT)
     weight = (1.0 - DECAY) / width
     sides = ((lf, left_gram, left_buf, left_out), (rf, right_gram, right_buf, right_out))
     for s in range(CAP):
@@ -365,6 +375,7 @@
         pltpu.make_async_copy(uall.at[buffer_of(pos & 3), pos >> 2], update.at[b], sems.at[1]).start()
         return carry
 
+    load.wait()
     lax.fori_loop(0, blocks, put, 0)
     pltpu.make_async_copy(left_buf, left_out, sems.at[2]).wait()
     pltpu.make_async_copy(right_buf, right_out, sems.at[2]).wait()
@@ -409,7 +420,7 @@
             pltpu.VMEM((width, width), bf16),
             [pltpu.VMEM((places, rows, part), bf16)] * CHUNKS,
             [pltpu.VMEM((places, rows, part), bf16)] * (CHUNKS * three),
-            [pltpu.VMEM((devs, rows, part), bf16)] * CHUNKS,
+            [pltpu.VMEM((devs, rows, (e - b) * width // BACK[-1]), bf16) for b, e in zip(BACK, BACK[1:])],
             dma((7,)),
             dma((CHUNKS, PIECES)),
             dma((CHUNKS, PIECES)),
@@ -421,10 +432,10 @@
             dma((CHUNKS, three)),
             dma((CHUNKS, PIECES)),
             dma((CHUNKS, PIECES)),
-            dma((CHUNKS,)),
-            dma((CHUNKS,)),
-            dma((CHUNKS, PIECES)),
-            dma((CHUNKS, PIECES)),
+            dma((len(BACK) - 1,)),
+            dma((len(BACK) - 1,)),
+            dma((len(BACK) - 1, PIECES)),
+            dma((len(BACK) - 1, PIECES)),
         ],
         compiler_params=pltpu.CompilerParams(
             collective_id=0, has_side_effects=True, vmem_limit_bytes=40 * 2**20
@@ -438,7 +449,7 @@
             jax.ShapeDtypeStruct((CAP, width, width), f32),
             jax.ShapeDtypeStruct((CAP, width, width), f32),
         ],
-        in_specs=[any_spec] + [vmem_spec] * 5,
+        in_specs=[vmem_spec] * 6,
         out_specs=[hbm_spec] * 3,
         scratch_shapes=[
             pltpu.SMEM((TAB_ROWS, 128), jnp.int32),
@@ -447,7 +458,7 @@
             dma((3,)),
         ],
         compiler_params=pltpu.CompilerParams(vmem_limit_bytes=24 * 2**20),
-    )(tab, *(from_vmem(x) for x in (left_gram, right_gram, uall, lf, rf)))
+    )(*(from_vmem(x) for x in (tab, left_gram, right_gram, uall, lf, rf)))
     return update, left_out, right_out
 
 

time: 51 us -> 50.1 us (0.982)
  Pallas kernels: 50.2 us -> 49.3 us
    pallas_call x1, Pallas kernels: 4.28 us -> 3.7 us  [shards(): pl.pallas_call(functools.partial(write_out, reps), name='write_out', out_...]
where the time goes in v5:
time: 50.1 us; the launch traced here: 49.9 us
  Pallas kernels  49.3 us (98%)
  between operations  0.64 us (1%)
    pallas_call x1, Pallas kernels, shards(): pl.pallas_call(functools.partial(exchange, reps, devs), name='exchange',...  45.6 us
    pallas_call x1, Pallas kernels, shards(): pl.pallas_call(functools.partial(write_out, reps), name='write_out', out_...  3.7 us

profile of v5, /device:TPU:1, one launch (start us, length us, event | category | flops | bytes accessed | tf_op | source)
XLA Modules:
  0.0 49.9 jit_solution(10833680288464018427)
XLA Ops:
  0.6 45.6 %exchange.1 = (s32[16,128]{1,0:T(8,128)S(1)}, f32[4,512,512]{2,1,0:T(8,128)S(1)}, f32[4,512,512]{2,1,0:T(8,128)S(1)}, bf16[4,16,16,512]{3,2,1,0:T(8,128)(2,1)S(1...) custom-call(s32[1,64]{1,0:T(1,128)} %bitcast.1, bf16[1,64,16,512]{3,2,1,0:T(8,128)(2,1)} %grad_hbm.1, ...), custom_call_target="tpu_custom_call" | custom-call | tf_op jit(solution)/shard_map/exchange/pallas_call | solution.py:395
  46.2 3.7 %write_out.1 = (bf16[64,16,512]{2,1,0:T(8,128)(2,1)}, f32[4,512,512]{2,1,0:T(8,128)}, f32[4,512,512]{2,1,0:T(8,128)}) custom-call(s32[16,128]{1,0:T(8,128)S(1)} %get-tuple-element.9.tab_v, f32[4,512,512]{2,1,0:T(8,128)S(1)} %get-tuple-element.10.left_gram, f32[4,512,512]{2,1,0:T(8,128)S(1)} %get-tuple-element.11.right_gram, ...), custom_call_target="tpu_custom_call" | custom-call | tf_op jit(solution)/shard_map/write_out/pallas_call | solution.py:444

commit v6 on v5

--- a/solution.py
+++ b/solution.py
@@ -276,14 +276,31 @@
 
     for c in range(1, CHUNKS):
         others(1 + c % 2, c)
-    others(3, 0)
-    for c in range(1, CHUNKS):
-        others(3, c)
+    for c in range(CHUNKS):
+        for p in (4, 5):
+            ag[c][p].wait_recv()
+    far = rep_of(reps - STEPS[2])
+
+    def to_far_owner(t, carry):
+        o = dp_peer(t)
+        place = tab[ROW_PLACE + far, o]
+        for c in range(CHUNKS):
+            stage[3, o, :, cols[c]] = s_recv[2 * CHUNKS + c][place]
+        one(stage.at[3, o], gath.at[3, mine, :], ot_ss.at[0, 2], ot_rs.at[0, 2], o)
+        return carry
+
+    for p in far_order():
+        to_far_owner(p, 0)
+    for c in range(CHUNKS):
+        gath[3, mine, cols[c]] = s_recv[2 * CHUNKS + c][tab[ROW_PLACE + far, d]]
 
     def gram(i):
-        if i > 0:
+        if i == 3:
+            arrived = gath.at[3, pl.ds(0, rows * (devs - 1)), :]
+            pltpu.make_async_copy(arrived, arrived, ot_rs.at[0, 2]).wait()
+        elif i > 0:
             for c in range(CHUNKS):
-                if i == 3 or i == 1 + c % 2:
+                if i == 1 + c % 2:
                     arrived = gath.at[i, pl.ds(0, rows * (devs - 1)), cols[c]]
                     pltpu.make_async_copy(arrived, arrived, ot_rs.at[c, i - 1]).wait()
                 else:
@@ -325,9 +342,11 @@
     for c in range(CHUNKS):
         for copy in list(rs[c].values()) + list(ag[c].values()) + [ow[c]]:
             copy.wait_send()
-        for i in (0, 1 + c % 2, 3):
+        for i in (0, 1 + c % 2):
             sent = stage.at[i, pl.ds(0, devs - 1), :, cols[c]]
             pltpu.make_async_copy(sent, sent, pr_ss.at[c] if i == 0 else ot_ss.at[c, i - 1]).wait()
+    sent = stage.at[3, pl.ds(0, devs - 1)]
+    pltpu.make_async_copy(sent, sent, ot_ss.at[0, 2]).wait()
     for c in range(len(bcols)):
         for copy in au[c].values():
             copy.wait_send()

time: 50.1 us -> 50 us (level)
  no operation moved by 1% of the time
where the time goes in v6:
time: 50 us; the launch traced here: 49.8 us
  Pallas kernels  49.2 us (98%)
  between operations  0.64 us (1%)
    pallas_call x1, Pallas kernels, shards(): pl.pallas_call(functools.partial(exchange, reps, devs), name='exchange',...  45.5 us
    pallas_call x1, Pallas kernels, shards(): pl.pallas_call(functools.partial(write_out, reps), name='write_out', out_...  3.7 us

profile of v6, /device:TPU:1, one launch (start us, length us, event | category | flops | bytes accessed | tf_op | source)
XLA Modules:
  0.0 49.8 jit_solution(4453181240484728996)
XLA Ops:
  0.6 45.5 %exchange.1 = (s32[16,128]{1,0:T(8,128)S(1)}, f32[4,512,512]{2,1,0:T(8,128)S(1)}, f32[4,512,512]{2,1,0:T(8,128)S(1)}, bf16[4,16,16,512]{3,2,1,0:T(8,128)(2,1)S(1...) custom-call(s32[1,64]{1,0:T(1,128)} %bitcast.1, bf16[1,64,16,512]{3,2,1,0:T(8,128)(2,1)} %grad_hbm.1, ...), custom_call_target="tpu_custom_call" | custom-call | tf_op jit(solution)/shard_map/exchange/pallas_call | solution.py:414
  46.1 3.7 %write_out.1 = (bf16[64,16,512]{2,1,0:T(8,128)(2,1)}, f32[4,512,512]{2,1,0:T(8,128)}, f32[4,512,512]{2,1,0:T(8,128)}) custom-call(s32[16,128]{1,0:T(8,128)S(1)} %get-tuple-element.9.tab_v, f32[4,512,512]{2,1,0:T(8,128)S(1)} %get-tuple-element.10.left_gram, f32[4,512,512]{2,1,0:T(8,128)S(1)} %get-tuple-element.11.right_gram, ...), custom_call_target="tpu_custom_call" | custom-call | tf_op jit(solution)/shard_map/write_out/pallas_call | solution.py:463

commit v7 on v6

--- a/solution.py
+++ b/solution.py
@@ -335,8 +335,8 @@
         if c > 0:
             pass_on(au[c - 1], steps(c - 1), au_ss.at[c - 1], au_rs.at[c - 1])
         au[c].update(share((2, 3), steps(c), au_ss.at[c], au_rs.at[c]))
+    gram(2)
     pass_on(au[-1], steps(len(bcols) - 1), au_ss.at[len(bcols) - 1], au_rs.at[len(bcols) - 1])
-    gram(2)
     gram(3)
 
     for c in range(CHUNKS):

time: 50 us -> 51 us (1.020); the launches traced: 49.8 us -> 50.1 us
  no operation moved by 1% of the time
where the time goes in v7:
time: 51 us; the launch traced here: 50.1 us
  Pallas kernels  49.5 us (97%)
  between operations  0.64 us (1%)
    pallas_call x1, Pallas kernels, shards(): pl.pallas_call(functools.partial(exchange, reps, devs), name='exchange',...  45.8 us
    pallas_call x1, Pallas kernels, shards(): pl.pallas_call(functools.partial(write_out, reps), name='write_out', out_...  3.7 us

profile of v7, /device:TPU:1, one launch (start us, length us, event | category | flops | bytes accessed | tf_op | source)
XLA Modules:
  0.0 50.1 jit_solution(15956010707565774696)
XLA Ops:
  0.6 45.8 %exchange.1 = (s32[16,128]{1,0:T(8,128)S(1)}, f32[4,512,512]{2,1,0:T(8,128)S(1)}, f32[4,512,512]{2,1,0:T(8,128)S(1)}, bf16[4,16,16,512]{3,2,1,0:T(8,128)(2,1)S(1...) custom-call(s32[1,64]{1,0:T(1,128)} %bitcast.1, bf16[1,64,16,512]{3,2,1,0:T(8,128)(2,1)} %grad_hbm.1, ...), custom_call_target="tpu_custom_call" | custom-call | tf_op jit(solution)/shard_map/exchange/pallas_call | solution.py:414
  46.4 3.7 %write_out.1 = (bf16[64,16,512]{2,1,0:T(8,128)(2,1)}, f32[4,512,512]{2,1,0:T(8,128)}, f32[4,512,512]{2,1,0:T(8,128)}) custom-call(s32[16,128]{1,0:T(8,128)S(1)} %get-tuple-element.9.tab_v, f32[4,512,512]{2,1,0:T(8,128)S(1)} %get-tuple-element.10.left_gram, f32[4,512,512]{2,1,0:T(8,128)S(1)} %get-tuple-element.11.right_gram, ...), custom_call_target="tpu_custom_call" | custom-call | tf_op jit(solution)/shard_map/write_out/pallas_call | solution.py:463
